TPU v7x, 32 devices: a whole 2x2x4 slice. The times are simulated.
32 devices in a mesh: shard: 8 (over z, x), ctx: 4 (over y, core).
Axes of the slice: x: 2, y: 2, z: 4, core: 2. Of those that a mesh axis runs over, the one named last changes fastest.
Arguments:
- inputs: bfloat16 [8, 768, 768], P('shard', 'ctx'), may hold values from -6 to 6
- encoder_states: bfloat16 [8, 512, 768], P('shard', 'ctx'), may hold values from -6 to 6
- cotangent: bfloat16 [8, 768, 768], P('shard', 'ctx'), may hold values from -6 to 6
- span_order: int32 [8], replicated, may hold values from 0 to 7, each once
- buckets: int32 [128], replicated, may hold values from 0 to 30, as said below
- gain_self: bfloat16 [768], P(('shard', 'ctx')), may hold values from 0.25 to 1.75
- self_query: bfloat16 [768, 768], P(('shard', 'ctx')), may hold values from -0.21875 to 0.21875
- self_key: bfloat16 [768, 768], P(('shard', 'ctx')), may hold values from -0.21875 to 0.21875
- self_value: bfloat16 [768, 768], P(('shard', 'ctx')), may hold values from -0.21875 to 0.21875
- self_out: bfloat16 [768, 768], P(('shard', 'ctx')), may hold values from -1.75 to 1.75
- gain_cross: bfloat16 [768], P(('shard', 'ctx')), may hold values from 0.25 to 1.75
- cross_query: bfloat16 [768, 768], P(('shard', 'ctx')), may hold values from -0.21875 to 0.21875
- cross_key: bfloat16 [768, 768], P(('shard', 'ctx')), may hold values from -0.21875 to 0.21875
- cross_value: bfloat16 [768, 768], P(('shard', 'ctx')), may hold values from -0.21875 to 0.21875
- cross_out: bfloat16 [768, 768], P(('shard', 'ctx')), may hold values from -1.75 to 1.75
- gain_feed: bfloat16 [768], P(('shard', 'ctx')), may hold values from 0.25 to 1.75
- feed_gate: bfloat16 [768, 2048], P(('shard', 'ctx')), may hold values from -0.21875 to 0.21875
- feed_up: bfloat16 [768, 2048], P(('shard', 'ctx')), may hold values from -0.21875 to 0.21875
- feed_down: bfloat16 [2048, 768], P(('shard', 'ctx')), may hold values from -0.125 to 0.125
- bias_table: float32 [32, 12], replicated, may hold values from -6 to 6
Outputs:
- outputs: bfloat16 [8, 768, 768], P('shard', 'ctx')
- input_grad: bfloat16 [8, 768, 768], P('shard', 'ctx')
- encoder_grad: bfloat16 [8, 512, 768], P('shard', 'ctx')
- gain_self_grad: float32 [768], P(('shard', 'ctx'))
- self_query_grad: float32 [768, 768], P(('shard', 'ctx'))
- self_key_grad: float32 [768, 768], P(('shard', 'ctx'))
- self_value_grad: float32 [768, 768], P(('shard', 'ctx'))
- self_out_grad: float32 [768, 768], P(('shard', 'ctx'))
- gain_cross_grad: float32 [768], P(('shard', 'ctx'))
- cross_query_grad: float32 [768, 768], P(('shard', 'ctx'))
- cross_key_grad: float32 [768, 768], P(('shard', 'ctx'))
- cross_value_grad: float32 [768, 768], P(('shard', 'ctx'))
- cross_out_grad: float32 [768, 768], P(('shard', 'ctx'))
- gain_feed_grad: float32 [768], P(('shard', 'ctx'))
- feed_gate_grad: float32 [768, 2048], P(('shard', 'ctx'))
- feed_up_grad: float32 [768, 2048], P(('shard', 'ctx'))
- feed_down_grad: float32 [2048, 768], P(('shard', 'ctx'))
- bias_table_grad: float32 [32, 12], replicated
Inputs may be any that keep to these rules, and one draw needn't show every extreme that they name: A permutation of the blocks: rows i * 96 to (i + 1) * 96 - 1 of every sequence hold the consecutive positions from span_order[i] * 96 on. A drawn monotone bucket map: buckets[0] is 0; each next entry is 1 or 2 higher until 30 is reached, then it stays there.
All inputs are finite; a program needn't handle non-finite values.
Results may differ from a plain program's by a relative error of at most 0.024.
Values may be sent and summed in bfloat16 or wider, within the bound.
No kernel may reach another device: no remote copies, remote signals or barrier semaphores. Data moves between devices by JAX's collectives and lax.ppermute only.
A program may use at most 192 MiB of HBM per device.

v0:
```python
import math

import jax
import jax.numpy as jnp
from jax import lax
from jax.sharding import PartitionSpec as P

EPSILON = 1e-06
MASKED = -1e30
PRECISE = lax.Precision.HIGHEST


def normed(values, gain):
    return values * lax.rsqrt(jnp.mean(values * values, axis=-1, keepdims=True) + EPSILON) * gain


def project(left, right):
    return jnp.dot(left, right, preferred_element_type=jnp.float32)


def project_back(grads, weight):
    return lax.dot_general(
        grads, weight, (((1,), (1,)), ((), ())), preferred_element_type=jnp.float32
    )


def outer_sum(left, grads):
    return lax.dot_general(
        left, grads, (((0,), (0,)), ((), ())), preferred_element_type=jnp.float32
    )


def split_heads(matrix, head_count):
    return matrix.reshape(matrix.shape[0], head_count, matrix.shape[1] // head_count)


def locate(span_order, first_row, row_total, span_rows):
    row_index = first_row + jnp.arange(row_total, dtype=jnp.int32)
    slot_index = row_index // span_rows
    span_slots = jnp.arange(span_order.shape[0], dtype=jnp.int32)
    chosen = jnp.sum(
        jnp.where(slot_index[:, None] == span_slots[None, :], span_order[None, :], 0), axis=1
    )
    return chosen * span_rows + row_index % span_rows


def bucket_edges(buckets, table_rows):
    levels = jnp.arange(1, table_rows, dtype=jnp.int32)
    return jnp.sum((buckets[None, :] < levels[:, None]).astype(jnp.int32), axis=1)


def scores_for(query_heads, query_pos, key_heads, key_pos, table, edges, score_scale):
    table_rows = table.shape[0]
    products = (
        jnp.einsum("qhd,khd->hqk", query_heads, key_heads, preferred_element_type=jnp.float32)
        * score_scale
    )
    offset = query_pos[:, None] - key_pos[None, :]
    bucket_index = jnp.sum((offset[:, :, None] >= edges[None, None, :]).astype(jnp.int32), axis=-1)
    onehot = (bucket_index[:, :, None] == jnp.arange(table_rows, dtype=jnp.int32)).astype(
        jnp.float32
    )
    bias = jnp.einsum("qkb,bh->hqk", onehot, table, precision=PRECISE)
    scores = jnp.where(offset >= 0, products + bias, MASKED)
    return (scores, onehot)


def key_block(matrix, block_start, block_size, head_count):
    return split_heads(lax.dynamic_slice_in_dim(matrix, block_start, block_size, 0), head_count)


def softmax_stats(query_heads, query_pos, keys_all, key_pos, table, edges, score_scale, block_size):
    head_count = query_heads.shape[1]
    query_count = query_heads.shape[0]

    def softmax_visit(running, block_start):
        running_max, exp_total = running
        key_heads = key_block(keys_all, block_start, block_size, head_count)
        key_place = lax.dynamic_slice_in_dim(key_pos, block_start, block_size, 0)
        scores, _ = scores_for(
            query_heads, query_pos, key_heads, key_place, table, edges, score_scale
        )
        highest = jnp.maximum(running_max, jnp.max(scores, axis=-1))
        exp_total = exp_total * jnp.exp(running_max - highest) + jnp.sum(
            jnp.exp(scores - highest[:, :, None]), axis=-1
        )
        return ((highest, exp_total), None)

    initial = (
        jnp.full((head_count, query_count), MASKED, jnp.float32),
        jnp.zeros((head_count, query_count), jnp.float32),
    )
    starts = jnp.arange(keys_all.shape[0] // block_size, dtype=jnp.int32) * block_size
    (running_max, exp_total), _ = lax.scan(softmax_visit, initial, starts)
    return running_max + jnp.log(exp_total)


def attend_values(
    query_heads,
    query_pos,
    keys_all,
    values_all,
    key_pos,
    table,
    edges,
    log_norm,
    score_scale,
    block_size,
):
    head_count = query_heads.shape[1]

    def attend_visit(sums, block_start):
        rounded_sum, extra_sum = sums
        key_heads = key_block(keys_all, block_start, block_size, head_count)
        value_heads = key_block(values_all, block_start, block_size, head_count)
        key_place = lax.dynamic_slice_in_dim(key_pos, block_start, block_size, 0)
        scores, _ = scores_for(
            query_heads, query_pos, key_heads, key_place, table, edges, score_scale
        )
        probs = jnp.exp(scores - log_norm[:, :, None])
        probs_low = probs.astype(jnp.bfloat16)
        remainder = (probs - probs_low.astype(jnp.float32)).astype(jnp.bfloat16)
        rounded_sum = rounded_sum + jnp.einsum(
            "hqk,khd->qhd", probs_low, value_heads, preferred_element_type=jnp.float32
        )
        extra_sum = extra_sum + jnp.einsum(
            "hqk,khd->qhd", remainder, value_heads, preferred_element_type=jnp.float32
        )
        return ((rounded_sum, extra_sum), None)

    zeros_like_out = jnp.zeros(query_heads.shape, jnp.float32)
    starts = jnp.arange(keys_all.shape[0] // block_size, dtype=jnp.int32) * block_size
    (rounded_sum, extra_sum), _ = lax.scan(attend_visit, (zeros_like_out, zeros_like_out), starts)
    return (rounded_sum, rounded_sum + extra_sum)


def self_backward(
    query_heads,
    grad_heads,
    query_pos,
    keys_all,
    values_all,
    key_pos,
    table,
    edges,
    log_norm,
    delta,
    score_scale,
    block_size,
):
    head_count = query_heads.shape[1]
    table_rows = table.shape[0]

    def self_visit(sums, block_start):
        grad_query, grad_table = sums
        key_heads = key_block(keys_all, block_start, block_size, head_count)
        value_heads = key_block(values_all, block_start, block_size, head_count)
        key_place = lax.dynamic_slice_in_dim(key_pos, block_start, block_size, 0)
        scores, onehot = scores_for(
            query_heads, query_pos, key_heads, key_place, table, edges, score_scale
        )
        probs = jnp.exp(scores - log_norm[:, :, None])
        grad_probs = jnp.einsum(
            "qhd,khd->hqk", grad_heads, value_heads, preferred_element_type=jnp.float32
        )
        grad_scores = (probs * (grad_probs - delta[:, :, None])).astype(jnp.bfloat16)
        grad_query = grad_query + jnp.einsum(
            "hqk,khd->qhd", grad_scores, key_heads, preferred_element_type=jnp.float32
        )
        grad_table = grad_table + jnp.einsum(
            "hqk,qkb->bh",
            grad_scores,
            onehot.astype(jnp.bfloat16),
            preferred_element_type=jnp.float32,
        )
        probs_low = probs.astype(jnp.bfloat16)
        grad_key = jnp.einsum(
            "hqk,qhd->khd", grad_scores, query_heads, preferred_element_type=jnp.float32
        )
        grad_value = jnp.einsum(
            "hqk,qhd->khd", probs_low, grad_heads, preferred_element_type=jnp.float32
        )
        return ((grad_query, grad_table), (grad_key, grad_value))

    initial = (
        jnp.zeros(query_heads.shape, jnp.float32),
        jnp.zeros((table_rows, head_count), jnp.float32),
    )
    starts = jnp.arange(keys_all.shape[0] // block_size, dtype=jnp.int32) * block_size
    return lax.scan(self_visit, initial, starts)


def per_device(
    inputs,
    encoder_states,
    cotangent,
    span_order,
    buckets,
    gain_self,
    self_query,
    self_key,
    self_value,
    self_out,
    gain_cross,
    cross_query,
    cross_key,
    cross_value,
    cross_out,
    gain_feed,
    feed_gate,
    feed_up,
    feed_down,
    bias_table,
):
    gathered = (
        lax.all_gather(gain_self, ("shard", "ctx"), axis=0, tiled=True),
        lax.all_gather(self_query, ("shard", "ctx"), axis=0, tiled=True),
        lax.all_gather(self_key, ("shard", "ctx"), axis=0, tiled=True),
        lax.all_gather(self_value, ("shard", "ctx"), axis=0, tiled=True),
        lax.all_gather(self_out, ("shard", "ctx"), axis=0, tiled=True),
        lax.all_gather(gain_cross, ("shard", "ctx"), axis=0, tiled=True),
        lax.all_gather(cross_query, ("shard", "ctx"), axis=0, tiled=True),
        lax.all_gather(cross_key, ("shard", "ctx"), axis=0, tiled=True),
        lax.all_gather(cross_value, ("shard", "ctx"), axis=0, tiled=True),
        lax.all_gather(cross_out, ("shard", "ctx"), axis=0, tiled=True),
        lax.all_gather(gain_feed, ("shard", "ctx"), axis=0, tiled=True),
        lax.all_gather(feed_gate, ("shard", "ctx"), axis=0, tiled=True),
        lax.all_gather(feed_up, ("shard", "ctx"), axis=0, tiled=True),
        lax.all_gather(feed_down, ("shard", "ctx"), axis=0, tiled=True),
    )
    (
        whole_gain_self,
        whole_self_query,
        whole_self_key,
        whole_self_value,
        whole_self_out,
        whole_gain_cross,
        whole_cross_query,
        whole_cross_key,
        whole_cross_value,
        whole_cross_out,
        whole_gain_feed,
        whole_feed_gate,
        whole_feed_up,
        whole_feed_down,
    ) = gathered
    token_rows = inputs.shape[1]
    width = inputs.shape[2]
    head_count = bias_table.shape[1]
    head_size = width // head_count
    table_rows = bias_table.shape[0]
    group_size = lax.axis_size("ctx")
    device_slot = lax.axis_index("ctx")
    seq_rows = token_rows * group_size
    span_rows = token_rows // 2
    block_size = math.gcd(512, seq_rows)
    score_scale = head_size ** (-0.5)
    query_pos = locate(span_order, device_slot * token_rows, token_rows, span_rows)
    key_pos = locate(span_order, 0, seq_rows, span_rows)
    edges = bucket_edges(buckets, table_rows)
    tokens = inputs[0].astype(jnp.float32)
    normed_self = normed(tokens, whole_gain_self.astype(jnp.float32)).astype(jnp.bfloat16)
    queries = project(normed_self, whole_self_query).astype(jnp.bfloat16)
    keys_local = project(normed_self, whole_self_key).astype(jnp.bfloat16)
    values_local = project(normed_self, whole_self_value).astype(jnp.bfloat16)
    keys_all, values_all = (
        lax.all_gather(keys_local, "ctx", axis=0, tiled=True),
        lax.all_gather(values_local, "ctx", axis=0, tiled=True),
    )
    query_heads = split_heads(queries, head_count)
    log_self = softmax_stats(
        query_heads, query_pos, keys_all, key_pos, bias_table, edges, score_scale, block_size
    )
    self_rounded, self_exact = attend_values(
        query_heads,
        query_pos,
        keys_all,
        values_all,
        key_pos,
        bias_table,
        edges,
        log_self,
        score_scale,
        block_size,
    )
    attended = self_rounded.reshape(token_rows, width).astype(jnp.bfloat16)
    after_self = tokens + project(attended, whole_self_out)
    normed_cross = normed(after_self, whole_gain_cross.astype(jnp.float32)).astype(jnp.bfloat16)
    cross_q = project(normed_cross, whole_cross_query).astype(jnp.bfloat16)
    encoded_local = encoder_states[0]
    encoded_all = lax.all_gather(encoded_local, "ctx", axis=0, tiled=True)
    cross_k = project(encoded_all, whole_cross_key).astype(jnp.bfloat16)
    cross_v = project(encoded_all, whole_cross_value).astype(jnp.bfloat16)
    cross_q_heads = split_heads(cross_q, head_count)
    cross_k_heads = split_heads(cross_k, head_count)
    cross_v_heads = split_heads(cross_v, head_count)
    cross_scores = (
        jnp.einsum("qhd,khd->hqk", cross_q_heads, cross_k_heads, preferred_element_type=jnp.float32)
        * score_scale
    )
    cross_top = jnp.max(cross_scores, axis=-1)
    log_cross = cross_top + jnp.log(jnp.sum(jnp.exp(cross_scores - cross_top[:, :, None]), axis=-1))
    cross_probs = jnp.exp(cross_scores - log_cross[:, :, None])
    cross_low = cross_probs.astype(jnp.bfloat16)
    cross_remainder = (cross_probs - cross_low.astype(jnp.float32)).astype(jnp.bfloat16)
    cross_rounded = jnp.einsum(
        "hqk,khd->qhd", cross_low, cross_v_heads, preferred_element_type=jnp.float32
    )
    cross_exact = cross_rounded + jnp.einsum(
        "hqk,khd->qhd", cross_remainder, cross_v_heads, preferred_element_type=jnp.float32
    )
    cross_att = cross_rounded.reshape(token_rows, width).astype(jnp.bfloat16)
    after_cross = after_self + project(cross_att, whole_cross_out)
    normed_feed = normed(after_cross, whole_gain_feed.astype(jnp.float32)).astype(jnp.bfloat16)
    gate_pre = project(normed_feed, whole_feed_gate)
    up_pre = project(normed_feed, whole_feed_up)
    gated, gated_pull = jax.vjp(
        lambda first, second: jax.nn.gelu(first, approximate=True) * second, gate_pre, up_pre
    )
    hidden = gated.astype(jnp.bfloat16)
    outputs = (after_cross + project(hidden, whole_feed_down)).astype(jnp.bfloat16)
    back_weights = (
        lax.all_gather(gain_self, ("shard", "ctx"), axis=0, tiled=True),
        lax.all_gather(self_query, ("shard", "ctx"), axis=0, tiled=True),
        lax.all_gather(self_key, ("shard", "ctx"), axis=0, tiled=True),
        lax.all_gather(self_value, ("shard", "ctx"), axis=0, tiled=True),
        lax.all_gather(self_out, ("shard", "ctx"), axis=0, tiled=True),
        lax.all_gather(gain_cross, ("shard", "ctx"), axis=0, tiled=True),
        lax.all_gather(cross_query, ("shard", "ctx"), axis=0, tiled=True),
        lax.all_gather(cross_key, ("shard", "ctx"), axis=0, tiled=True),
        lax.all_gather(cross_value, ("shard", "ctx"), axis=0, tiled=True),
        lax.all_gather(cross_out, ("shard", "ctx"), axis=0, tiled=True),
        lax.all_gather(gain_feed, ("shard", "ctx"), axis=0, tiled=True),
        lax.all_gather(feed_gate, ("shard", "ctx"), axis=0, tiled=True),
        lax.all_gather(feed_up, ("shard", "ctx"), axis=0, tiled=True),
        lax.all_gather(feed_down, ("shard", "ctx"), axis=0, tiled=True),
    )
    (
        back_gain_self,
        back_self_query,
        back_self_key,
        back_self_value,
        back_self_out,
        back_gain_cross,
        back_cross_query,
        back_cross_key,
        back_cross_value,
        back_cross_out,
        back_gain_feed,
        back_feed_gate,
        back_feed_up,
        back_feed_down,
    ) = back_weights
    outer = cotangent[0].astype(jnp.float32)
    grad_feed_out = outer.astype(jnp.bfloat16)
    down_grad = outer_sum(hidden, grad_feed_out)
    grad_hidden = project_back(grad_feed_out, back_feed_down)
    grad_gate_f, grad_up_f = gated_pull(grad_hidden)
    grad_gate = grad_gate_f.astype(jnp.bfloat16)
    grad_up = grad_up_f.astype(jnp.bfloat16)
    gate_grad = outer_sum(normed_feed, grad_gate)
    up_grad = outer_sum(normed_feed, grad_up)
    grad_normed_feed = project_back(grad_gate, back_feed_gate) + project_back(grad_up, back_feed_up)
    _, feed_norm_pull = jax.vjp(normed, after_cross, back_gain_feed.astype(jnp.float32))
    grad_after_feed, gain_feed_grad = feed_norm_pull(grad_normed_feed)
    grad_after_cross = outer + grad_after_feed
    grad_cross_branch = grad_after_cross.astype(jnp.bfloat16)
    cross_out_grad = outer_sum(cross_att, grad_cross_branch)
    grad_cross_att = project_back(grad_cross_branch, back_cross_out).astype(jnp.bfloat16)
    grad_cross_heads = split_heads(grad_cross_att, head_count)
    cross_delta = jnp.sum(
        (grad_cross_att.astype(jnp.float32) * cross_exact.reshape(token_rows, width)).reshape(
            token_rows, head_count, head_size
        ),
        axis=-1,
    ).T
    cross_grad_probs = jnp.einsum(
        "qhd,khd->hqk", grad_cross_heads, cross_v_heads, preferred_element_type=jnp.float32
    )
    cross_grad_scores = (cross_probs * (cross_grad_probs - cross_delta[:, :, None])).astype(
        jnp.bfloat16
    )
    grad_cross_q = (
        (
            jnp.einsum(
                "hqk,khd->qhd", cross_grad_scores, cross_k_heads, preferred_element_type=jnp.float32
            )
            * score_scale
        )
        .reshape(token_rows, width)
        .astype(jnp.bfloat16)
    )
    part_cross_k = (
        jnp.einsum(
            "hqk,qhd->khd", cross_grad_scores, cross_q_heads, preferred_element_type=jnp.float32
        )
        * score_scale
    ).reshape(-1, width)
    part_cross_v = jnp.einsum(
        "hqk,qhd->khd", cross_low, grad_cross_heads, preferred_element_type=jnp.float32
    ).reshape(-1, width)
    summed_cross_k, summed_cross_v = (
        lax.psum_scatter(
            part_cross_k.astype(jnp.bfloat16), "ctx", scatter_dimension=0, tiled=True
        ).astype(jnp.float32),
        lax.psum_scatter(
            part_cross_v.astype(jnp.bfloat16), "ctx", scatter_dimension=0, tiled=True
        ).astype(jnp.float32),
    )
    grad_cross_k = summed_cross_k.astype(jnp.bfloat16)
    grad_cross_v = summed_cross_v.astype(jnp.bfloat16)
    cross_key_grad = outer_sum(encoded_local, grad_cross_k)
    cross_value_grad = outer_sum(encoded_local, grad_cross_v)
    encoder_grad = (
        project_back(grad_cross_k, back_cross_key) + project_back(grad_cross_v, back_cross_value)
    ).astype(jnp.bfloat16)
    cross_query_grad = outer_sum(normed_cross, grad_cross_q)
    grad_normed_cross = project_back(grad_cross_q, back_cross_query)
    _, cross_norm_pull = jax.vjp(normed, after_self, back_gain_cross.astype(jnp.float32))
    grad_after_norm, gain_cross_grad = cross_norm_pull(grad_normed_cross)
    grad_after_self = grad_after_cross + grad_after_norm
    grad_self_branch = grad_after_self.astype(jnp.bfloat16)
    self_out_grad = outer_sum(attended, grad_self_branch)
    grad_attended = project_back(grad_self_branch, back_self_out).astype(jnp.bfloat16)
    grad_heads = split_heads(grad_attended, head_count)
    self_delta = jnp.sum(
        (grad_attended.astype(jnp.float32) * self_exact.reshape(token_rows, width)).reshape(
            token_rows, head_count, head_size
        ),
        axis=-1,
    ).T
    (grad_query_f, table_part), stacked = self_backward(
        query_heads,
        grad_heads,
        query_pos,
        keys_all,
        values_all,
        key_pos,
        bias_table,
        edges,
        log_self,
        self_delta,
        score_scale,
        block_size,
    )
    part_keys = (stacked[0] * score_scale).reshape(seq_rows, width)
    part_values = stacked[1].reshape(seq_rows, width)
    summed_key, summed_value = (
        lax.psum_scatter(
            part_keys.astype(jnp.bfloat16), "ctx", scatter_dimension=0, tiled=True
        ).astype(jnp.float32),
        lax.psum_scatter(
            part_values.astype(jnp.bfloat16), "ctx", scatter_dimension=0, tiled=True
        ).astype(jnp.float32),
    )
    grad_query = (grad_query_f * score_scale).reshape(token_rows, width).astype(jnp.bfloat16)
    grad_key = summed_key.astype(jnp.bfloat16)
    grad_value = summed_value.astype(jnp.bfloat16)
    query_grad = outer_sum(normed_self, grad_query)
    key_grad = outer_sum(normed_self, grad_key)
    value_grad = outer_sum(normed_self, grad_value)
    grad_normed_self = (
        project_back(grad_query, back_self_query)
        + project_back(grad_key, back_self_key)
        + project_back(grad_value, back_self_value)
    )
    _, self_norm_pull = jax.vjp(normed, tokens, back_gain_self.astype(jnp.float32))
    grad_tokens_norm, gain_self_grad = self_norm_pull(grad_normed_self)
    input_grad = (grad_after_self + grad_tokens_norm).astype(jnp.bfloat16)
    reduced = (
        lax.psum_scatter(gain_self_grad, ("shard", "ctx"), scatter_dimension=0, tiled=True),
        lax.psum_scatter(query_grad, ("shard", "ctx"), scatter_dimension=0, tiled=True),
        lax.psum_scatter(key_grad, ("shard", "ctx"), scatter_dimension=0, tiled=True),
        lax.psum_scatter(value_grad, ("shard", "ctx"), scatter_dimension=0, tiled=True),
        lax.psum_scatter(self_out_grad, ("shard", "ctx"), scatter_dimension=0, tiled=True),
        lax.psum_scatter(gain_cross_grad, ("shard", "ctx"), scatter_dimension=0, tiled=True),
        lax.psum_scatter(cross_query_grad, ("shard", "ctx"), scatter_dimension=0, tiled=True),
        lax.psum_scatter(cross_key_grad, ("shard", "ctx"), scatter_dimension=0, tiled=True),
        lax.psum_scatter(cross_value_grad, ("shard", "ctx"), scatter_dimension=0, tiled=True),
        lax.psum_scatter(cross_out_grad, ("shard", "ctx"), scatter_dimension=0, tiled=True),
        lax.psum_scatter(gain_feed_grad, ("shard", "ctx"), scatter_dimension=0, tiled=True),
        lax.psum_scatter(gate_grad, ("shard", "ctx"), scatter_dimension=0, tiled=True),
        lax.psum_scatter(up_grad, ("shard", "ctx"), scatter_dimension=0, tiled=True),
        lax.psum_scatter(down_grad, ("shard", "ctx"), scatter_dimension=0, tiled=True),
    )
    table_total = lax.psum(table_part, ("shard", "ctx"))
    return (
        outputs[None],
        input_grad[None],
        encoder_grad[None],
        reduced[0],
        reduced[1],
        reduced[2],
        reduced[3],
        reduced[4],
        reduced[5],
        reduced[6],
        reduced[7],
        reduced[8],
        reduced[9],
        reduced[10],
        reduced[11],
        reduced[12],
        reduced[13],
        table_total,
    )


def solution(mesh):
    in_specs = (
        P("shard", "ctx", None),
        P("shard", "ctx", None),
        P("shard", "ctx", None),
        P(),
        P(),
        P(("shard", "ctx")),
        P(("shard", "ctx"), None),
        P(("shard", "ctx"), None),
        P(("shard", "ctx"), None),
        P(("shard", "ctx"), None),
        P(("shard", "ctx")),
        P(("shard", "ctx"), None),
        P(("shard", "ctx"), None),
        P(("shard", "ctx"), None),
        P(("shard", "ctx"), None),
        P(("shard", "ctx")),
        P(("shard", "ctx"), None),
        P(("shard", "ctx"), None),
        P(("shard", "ctx"), None),
        P(),
    )
    out_specs = (
        P("shard", "ctx", None),
        P("shard", "ctx", None),
        P("shard", "ctx", None),
        P(("shard", "ctx")),
        P(("shard", "ctx"), None),
        P(("shard", "ctx"), None),
        P(("shard", "ctx"), None),
        P(("shard", "ctx"), None),
        P(("shard", "ctx")),
        P(("shard", "ctx"), None),
        P(("shard", "ctx"), None),
        P(("shard", "ctx"), None),
        P(("shard", "ctx"), None),
        P(("shard", "ctx")),
        P(("shard", "ctx"), None),
        P(("shard", "ctx"), None),
        P(("shard", "ctx"), None),
        P(),
    )
    return jax.shard_map(
        per_device, mesh=mesh, in_specs=in_specs, out_specs=out_specs, check_vma=False
    )
```

profile of v0, /device:TPU:0, one launch (start us, length us, event | category | flops | bytes accessed | tf_op | source)
XLA Modules:
  0.0 2039.1 jit_solution(5921538554963519725)
XLA Ops:
  13.2 42.1 %all-reduce.7 = (bf16[768]{0:T(1024)(128)(2,1)S(1)}, bf16[768]{0:T(1024)(128)(2,1)S(1)}, bf16[768]{0:T(1024)(128)(2,1)S(1)}) all-reduce(bf16[768]{0:T(1024)(128)(2,1)S(1)} %dynamic-update-slice, bf16[768]{0:T(1024)(128)(2,1)S(1)} %dynamic-update-slice.1, ...), channel_id=1, replica_groups=mesh['shard'=8,'ctx'=4] {'shard','ctx'}, use_global_device_ids=true, to_apply=%add | all-reduce | flops 2304 | bytes 9216
  57.0 10.9 all-gather.19.cloned.1.call-done
  70.4 53.4 %all-gather.15.cloned.1.call-done = bf16[768,768]{1,0:T(8,128)(2,1)} async-done(((bf16[24,768]{1,0:T(8,128)(2,1)}), bf16[768,768]{1,0:T(8,128)(2,1)}) %all-gather.15.cloned.1.call-update) | async-done | bytes 1179664 | tf_op jit(solution)/shard_map/all_gather | solution.py:219
  130.8 9.2 all-gather
  140.2 39.6 %all-gather.23.cloned.1.call-done = bf16[768,768]{1,0:T(8,128)(2,1)} async-done(((bf16[24,768]{1,0:T(8,128)(2,1)}), bf16[768,768]{1,0:T(8,128)(2,1)}) %all-gather.23.cloned.1.call-update) | async-done | bytes 1179664 | tf_op jit(solution)/shard_map/all_gather | solution.py:217
  181.7 53.9 %all-gather.31.cloned.1.call-done = bf16[768,768]{1,0:T(8,128)(2,1)} async-done(((bf16[24,768]{1,0:T(8,128)(2,1)}), bf16[768,768]{1,0:T(8,128)(2,1)}) %all-gather.31.cloned.1.call-update) | async-done | bytes 1179664 | tf_op jit(solution)/shard_map/all_gather | solution.py:223
  238.8 52.6 %all-gather.27.cloned.1.call-done = bf16[768,768]{1,0:T(8,128)(2,1)} async-done(((bf16[24,768]{1,0:T(8,128)(2,1)}), bf16[768,768]{1,0:T(8,128)(2,1)}) %all-gather.27.cloned.1.call-update) | async-done | bytes 1179664 | tf_op jit(solution)/shard_map/all_gather | solution.py:224
  294.7 15.2 all-gather.21.cloned.1.call-done
  312.2 29.5 %while.43 = (s32[]{:T(128)}, f32[12,192]{1,0:T(8,128)S(1)}, f32[12,192]{1,0:T(8,128)S(1)}, s32[192]{0:T(256)S(1)}, s32[3]{0:T(128)S(1)}, /*index=5*/s32[768]{0:T...) while((s32[]{:T(128)}, f32[12,192]{1,0:T(8,128)S(1)}, ...), condition=%wide.region_8.9_spmd.clone, body=%wide.region_4.8_spmd.clone.sunk | while | flops 311782656 | bytes 11923770 | solution.py:94
  344.1 41.5 %while.44 = (s32[]{:T(128)}, f32[192,12,64]{0,2,1:T(8,128)}, f32[192,12,64]{0,2,1:T(8,128)}, s32[3]{0:T(128)S(1)}, bf16[768,768]{0,1:T(8,128)(2,1)}, /*index=5*/...) while((s32[]{:T(128)}, f32[192,12,64]{0,2,1:T(8,128)}, ...), condition=%wide.region_11.12_spmd.clone, body=%wide.region_9.11_spmd.clone.sunk | while | flops 465125376 | bytes 18104648 | solution.py:133
  385.6 2.7 fusion.118
  390.4 52.1 %all-gather.29.cloned.1.call-done = bf16[768,768]{1,0:T(8,128)(2,1)} async-done(((bf16[24,768]{1,0:T(8,128)(2,1)}), bf16[768,768]{1,0:T(8,128)(2,1)}) %all-gather.29.cloned.1.call-update) | async-done | bytes 1179664 | tf_op jit(solution)/shard_map/all_gather | solution.py:222
  455.4 42.9 %all-gather.33.cloned.1.call-done = bf16[768,768]{1,0:T(8,128)(2,1)} async-done(((bf16[24,768]{1,0:T(8,128)(2,1)}), bf16[768,768]{1,0:T(8,128)(2,1)}) %all-gather.33.cloned.1.call-update) | async-done | bytes 1179664 | tf_op jit(solution)/shard_map/all_gather | solution.py:225
  500.3 59.0 %all-gather.35.cloned.1.call-done = bf16[768,2048]{1,0:T(8,128)(2,1)} async-done(((bf16[24,2048]{1,0:T(8,128)(2,1)}), bf16[768,2048]{1,0:T(8,128)(2,1)}) %all-gather.35.cloned.1.call-update) | async-done | bytes 3145744 | tf_op jit(solution)/shard_map/all_gather | solution.py:227
  559.2 3.8 fusion.120
  563.1 56.8 %all-gather.37.cloned.1.call-done = bf16[768,2048]{1,0:T(8,128)(2,1)} async-done(((bf16[24,2048]{1,0:T(8,128)(2,1)}), bf16[768,2048]{1,0:T(8,128)(2,1)}) %all-gather.37.cloned.1.call-update) | async-done | bytes 3145744 | tf_op jit(solution)/shard_map/all_gather | solution.py:228
  619.9 3.8 fusion.121
  623.7 57.0 %all-gather.39.cloned.1.call-done = bf16[2048,768]{1,0:T(8,128)(2,1)} async-done(((bf16[64,768]{1,0:T(8,128)(2,1)}), bf16[2048,768]{1,0:T(8,128)(2,1)}) %all-gather.39.cloned.1.call-update) | async-done | bytes 3145744 | tf_op jit(solution)/shard_map/all_gather | solution.py:229
  680.7 5.9 multiply_convert_fusion.3
  695.0 3.5 convolution_convert_fusion.2
  701.2 4.3 multiply_convert_fusion
  720.7 53.4 %while.45 = (s32[]{:T(128)}, f32[192,12,64]{0,2,1:T(8,128)}, f32[32,12]{0,1:T(8,128)}, f32[3,256,12,64]{1,3,2,0:T(8,128)}, bf16[3,256,12,64]{1,3,2,0:T(8,128)(2,...) while((s32[]{:T(128)}, f32[192,12,64]{0,2,1:T(8,128)}, ...), condition=%wide.region_22.23_spmd.clone, body=%wide.region_20.22_spmd.clone.sunk | while | flops 657703680 | bytes 32367576 | solution.py:190
  750.9 2.7 fusion.267
  768.7 2.7 fusion.267
  774.1 3.0 multiply_convert_fusion.1
  777.1 3.9 copy.145
  781.0 2.8 reshape.324
  783.9 5.0 copy.146
  788.9 4.9 reshape.326
  810.4 3.0 fusion.112
  813.5 23.4 %reduce-scatter.48.cloned.1.call-done = bf16[192,768]{1,0:T(8,128)(2,1)} async-done(((bf16[768,768]{1,0:T(8,128)(2,1)}), bf16[192,768]{1,0:T(8,128)(2,1)}) %reduce-scatter.48.cloned.1.call-update) | async-done | bytes 294928
  836.8 3.0 fusion.110
  839.9 3.7 fusion.125
  844.7 3.7 fusion.126
  849.7 3.6 fusion.78
  855.3 3.6 fusion.50
  862.1 39.9 %all-reduce.6 = (f32[768]{0:T(1024)S(1)}, f32[768]{0:T(1024)S(1)}, f32[768]{0:T(1024)S(1)}, f32[32,12]{0,1:T(8,128)}) all-reduce(f32[768]{0:T(1024)S(1)} %get-tuple-element.578, f32[768]{0:T(1024)S(1)} %copy-done.81, f32[768]{0:T(1024)S(1)} %copy-done.82, ...), channel_id=7, replica_groups=mesh['shard'=8,'ctx'=4] {'shard','ctx'}, use_global_device_ids=true, to_apply=%region_29.30.clone | all-reduce | flops 2688 | bytes 21504
  904.6 36.9 %reduce-scatter.36.cloned.1.call-done = f32[24,768]{1,0:T(8,128)} async-done(((f32[768,768]{1,0:T(8,128)}), f32[24,768]{1,0:T(8,128)}) %reduce-scatter.36.cloned.1.call-update) | async-done | bytes 73744 | tf_op jit(solution)/shard_map/reduce_scatter | solution.py:477
  941.6 104.8 %reduce-scatter.38.cloned.1.call-done = f32[24,768]{1,0:T(8,128)} async-done(((f32[768,768]{1,0:T(8,128)}), f32[24,768]{1,0:T(8,128)}) %reduce-scatter.38.cloned.1.call-update) | async-done | bytes 73744 | tf_op jit(solution)/shard_map/reduce_scatter | solution.py:480
  1046.4 103.7 %reduce-scatter.28.cloned.1.call-done = f32[24,768]{1,0:T(8,128)} async-done(((f32[768,768]{1,0:T(8,128)}), f32[24,768]{1,0:T(8,128)}) %reduce-scatter.28.cloned.1.call-update) | async-done | bytes 73744 | tf_op jit(solution)/shard_map/reduce_scatter | solution.py:472
  1150.1 104.8 %reduce-scatter.34.cloned.1.call-done = f32[24,768]{1,0:T(8,128)} async-done(((f32[768,768]{1,0:T(8,128)}), f32[24,768]{1,0:T(8,128)}) %reduce-scatter.34.cloned.1.call-update) | async-done | bytes 73744 | tf_op jit(solution)/shard_map/reduce_scatter | solution.py:475
  1254.9 103.9 %reduce-scatter.56.cloned.1.call-done = f32[24,768]{1,0:T(8,128)} async-done(((f32[768,768]{1,0:T(8,128)}), f32[24,768]{1,0:T(8,128)}) %reduce-scatter.56.cloned.1.call-update) | async-done | bytes 73744
  1358.8 104.8 %reduce-scatter.54.cloned.1.call-done = f32[24,768]{1,0:T(8,128)} async-done(((f32[768,768]{1,0:T(8,128)}), f32[24,768]{1,0:T(8,128)}) %reduce-scatter.54.cloned.1.call-update) | async-done | bytes 73744
  1463.6 103.8 %reduce-scatter.30.cloned.1.call-done = f32[24,768]{1,0:T(8,128)} async-done(((f32[768,768]{1,0:T(8,128)}), f32[24,768]{1,0:T(8,128)}) %reduce-scatter.30.cloned.1.call-update) | async-done | bytes 73744 | tf_op jit(solution)/shard_map/reduce_scatter | solution.py:473
  1567.3 104.8 %reduce-scatter.32.cloned.1.call-done = f32[24,768]{1,0:T(8,128)} async-done(((f32[768,768]{1,0:T(8,128)}), f32[24,768]{1,0:T(8,128)}) %reduce-scatter.32.cloned.1.call-update) | async-done | bytes 73744 | tf_op jit(solution)/shard_map/reduce_scatter | solution.py:474
  1672.1 119.4 %reduce-scatter.40.cloned.1.call-done = f32[24,2048]{1,0:T(8,128)} async-done(((f32[768,2048]{1,0:T(8,128)}), f32[24,2048]{1,0:T(8,128)}) %reduce-scatter.40.cloned.1.call-update) | async-done | bytes 196624 | tf_op jit(solution)/shard_map/reduce_scatter | solution.py:482
  1791.6 120.5 %reduce-scatter.42.cloned.1.call-done = f32[24,2048]{1,0:T(8,128)} async-done(((f32[768,2048]{1,0:T(8,128)}), f32[24,2048]{1,0:T(8,128)}) %reduce-scatter.42.cloned.1.call-update) | async-done | bytes 196624 | tf_op jit(solution)/shard_map/reduce_scatter | solution.py:483
  1912.1 119.7 %reduce-scatter.44.cloned.1.call-done = f32[64,768]{1,0:T(8,128)} async-done(((f32[2048,768]{1,0:T(8,128)}), f32[64,768]{1,0:T(8,128)}) %reduce-scatter.44.cloned.1.call-update) | async-done | bytes 196624 | tf_op jit(solution)/shard_map/reduce_scatter | solution.py:484
  (519 shorter events, 199.5 us)
Async XLA Ops:
  7.2 116.6 %copy-start.13 = (bf16[1,192,768]{2,1,0:T(8,128)(2,1)S(1)}, bf16[1,192,768]{2,1,0:T(8,128)(2,1)}, u32[]{:S(2)}) copy-start(bf16[1,192,768]{2,1,0:T(8,128)(2,1)} %param.26) | copy-start | bytes 884740
  7.2 60.6 %all-gather.19.cloned.1.call-start = ((), (), s32[]{:S(2)}) async-start(), calls=%async_computation.17 | async-start | bytes 1216512 | tf_op jit(solution)/shard_map/all_gather | solution.py:218
  7.9 115.8 %all-gather.15.cloned.1.call-start = ((), (), s32[]{:S(2)}) async-start(), calls=%async_computation.15 | async-start | bytes 1216512 | tf_op jit(solution)/shard_map/all_gather | solution.py:219
  8.7 171.1 %all-gather.23.cloned.1.call-start = ((), (), s32[]{:S(2)}) async-start(), calls=%async_computation.19 | async-start | bytes 1216512 | tf_op jit(solution)/shard_map/all_gather | solution.py:217
  9.4 226.2 %all-gather.31.cloned.1.call-start = ((), (), s32[]{:S(2)}) async-start(), calls=%async_computation.23 | async-start | bytes 1216512 | tf_op jit(solution)/shard_map/all_gather | solution.py:223
  10.0 281.4 %all-gather.27.cloned.1.call-start = ((), (), s32[]{:S(2)}) async-start(), calls=%async_computation.21 | async-start | bytes 1216512 | tf_op jit(solution)/shard_map/all_gather | solution.py:224
  10.6 299.3 %all-gather.21.cloned.1.call-start = ((), (), s32[]{:S(2)}) async-start(), calls=%async_computation.18 | async-start | bytes 1474560 | tf_op jit(solution)/shard_map/all_gather | solution.py:267
  55.3 124.5 %copy-start.69 = (f32[768]{0:T(1024)}, f32[768]{0:T(1024)S(1)}, u32[]{:S(2)}) copy-start(f32[768]{0:T(1024)S(1)} %convert_element_type.211) | copy-start | bytes 9220
  56.9 73.6 %copy-start.88 = (s32[8]{0:T(128)S(1)}, s32[8]{0:T(128)}, u32[]{:S(2)}) copy-start(s32[8]{0:T(128)} %param.29) | copy-start | bytes 100
  56.9 122.9 %copy-start.77 = (f32[192]{0:T(256)}, f32[192]{0:T(256)S(1)}, u32[]{:S(2)}) copy-start(f32[192]{0:T(256)S(1)} %fusion.103) | copy-start | bytes 2308
  57.0 73.8 %copy-start.53 = (bf16[1,128,768]{2,1,0:T(8,128)(2,1)S(1)}, bf16[1,128,768]{2,1,0:T(8,128)(2,1)}, u32[]{:S(2)}) copy-start(bf16[1,128,768]{2,1,0:T(8,128)(2,1)} %param.27) | copy-start | bytes 589828
  70.4 69.7 %copy-start.89 = (s32[128]{0:T(128)S(1)}, s32[128]{0:T(128)}, u32[]{:S(2)}) copy-start(s32[128]{0:T(128)} %param.30) | copy-start | bytes 1540
  70.4 271.4 %all-gather.17.cloned.1.call-start = ((), (), s32[]{:S(2)}) async-start(), calls=%async_computation.16 | async-start | bytes 1474560 | tf_op jit(solution)/shard_map/all_gather | solution.py:268
  126.2 262.1 %all-gather.25.cloned.1.call-start = ((), (), s32[]{:S(2)}) async-start(), calls=%async_computation.20 | async-start | bytes 1216512 | tf_op jit(solution)/shard_map/all_gather | solution.py:220
  127.0 315.5 %all-gather.29.cloned.1.call-start = ((), (), s32[]{:S(2)}) async-start(), calls=%async_computation.22 | async-start | bytes 1216512 | tf_op jit(solution)/shard_map/all_gather | solution.py:222
  127.7 370.6 %all-gather.33.cloned.1.call-start = ((), (), s32[]{:S(2)}) async-start(), calls=%async_computation.24 | async-start | bytes 1216512 | tf_op jit(solution)/shard_map/all_gather | solution.py:225
  128.3 430.9 %all-gather.35.cloned.1.call-start = ((), (), s32[]{:S(2)}) async-start(), calls=%async_computation.25 | async-start | bytes 3244032 | tf_op jit(solution)/shard_map/all_gather | solution.py:227
  129.1 490.8 %all-gather.37.cloned.1.call-start = ((), (), s32[]{:S(2)}) async-start(), calls=%async_computation.26 | async-start | bytes 3244032 | tf_op jit(solution)/shard_map/all_gather | solution.py:228
  129.6 551.0 %all-gather.39.cloned.1.call-start = ((), (), s32[]{:S(2)}) async-start(), calls=%async_computation.27 | async-start | bytes 3244032 | tf_op jit(solution)/shard_map/all_gather | solution.py:229
  130.4 673.1 %reduce-scatter.52.cloned.1.call-start = ((), (), s32[]{:S(2)}) async-start(), calls=%async_computation.40 | async-start | bytes 983040
  130.8 577.4 %copy-start.73 = (f32[768]{0:T(1024)}, f32[768]{0:T(1024)S(1)}, u32[]{:S(2)}) copy-start(f32[768]{0:T(1024)S(1)} %convert_element_type.220) | copy-start | bytes 9220
  293.5 18.7 copy-start.50
  388.3 54.2 %copy-start.40 = (bf16[192,12,64]{0,2,1:T(8,128)(2,1)}, bf16[192,12,64]{0,2,1:T(8,128)(2,1)S(1)}, u32[]{:S(2)}) copy-start(bf16[192,12,64]{0,2,1:T(8,128)(2,1)S(1)} %get-tuple-element.673) | copy-start | bytes 884740
  388.3 56.1 %copy-start.27 = (bf16[512,768]{0,1:T(8,128)(2,1)S(1)}, bf16[512,768]{0,1:T(8,128)(2,1)}, u32[]{:S(2)}) copy-start(bf16[512,768]{0,1:T(8,128)(2,1)} %copy.120) | copy-start | bytes 2359300
  390.3 317.8 %copy-start.7 = (f32[192,768]{1,0:T(8,128)}, f32[192,768]{1,0:T(8,128)S(1)}, u32[]{:S(2)}) copy-start(f32[192,768]{1,0:T(8,128)S(1)} %get-tuple-element.675) | copy-start | bytes 1769476
  390.3 317.8 %copy-start.79 = (f32[192]{0:T(256)}, f32[192]{0:T(256)S(1)}, u32[]{:S(2)}) copy-start(f32[192]{0:T(256)S(1)} %fusion.104) | copy-start | bytes 2308
  448.8 49.5 %copy-start.34 = (bf16[12,64,192]{2,1,0:T(8,128)(2,1)}, bf16[12,64,192]{2,1,0:T(8,128)(2,1)S(1)}, u32[]{:S(2)}) copy-start(bf16[12,64,192]{2,1,0:T(8,128)(2,1)S(1)} %get-tuple-element.678) | copy-start | bytes 884740
  500.1 190.9 %copy-start.11 = (f32[192,768]{1,0:T(8,128)}, f32[192,768]{1,0:T(8,128)S(1)}, u32[]{:S(2)}) copy-start(f32[192,768]{1,0:T(8,128)S(1)} %get-tuple-element.681) | copy-start | bytes 1769476
  500.3 119.6 %copy-start.19 = (bf16[192,768]{1,0:T(8,128)(2,1)}, bf16[192,768]{1,0:T(8,128)(2,1)S(1)}, u32[]{:S(2)}) copy-start(bf16[192,768]{1,0:T(8,128)(2,1)S(1)} %multiply_convert_fusion.6) | copy-start | bytes 884740
  699.7 107.2 %reduce-scatter.50.cloned.1.call-start = ((), (), s32[]{:S(2)}) async-start(), calls=%async_computation.39 | async-start | bytes 983040
  709.3 7.4 copy-start.39
  720.4 90.0 %reduce-scatter.46.cloned.1.call-start = ((), (), s32[]{:S(2)}) async-start(), calls=%async_computation.37 | async-start | bytes 1474560
  783.8 53.0 %reduce-scatter.48.cloned.1.call-start = ((), (), s32[]{:S(2)}) async-start(), calls=%async_computation.38 | async-start | bytes 1474560
  793.9 147.7 %reduce-scatter.36.cloned.1.call-start = ((), (), s32[]{:S(2)}) async-start(), calls=%async_computation.32 | async-start | bytes 2433024 | tf_op jit(solution)/shard_map/reduce_scatter | solution.py:477
  796.1 250.3 %reduce-scatter.38.cloned.1.call-start = ((), (), s32[]{:S(2)}) async-start(), calls=%async_computation.33 | async-start | bytes 2433024 | tf_op jit(solution)/shard_map/reduce_scatter | solution.py:480
  798.1 352.0 %reduce-scatter.28.cloned.1.call-start = ((), (), s32[]{:S(2)}) async-start(), calls=%async_computation.28 | async-start | bytes 2433024 | tf_op jit(solution)/shard_map/reduce_scatter | solution.py:472
  801.4 453.5 %reduce-scatter.34.cloned.1.call-start = ((), (), s32[]{:S(2)}) async-start(), calls=%async_computation.31 | async-start | bytes 2433024 | tf_op jit(solution)/shard_map/reduce_scatter | solution.py:475
  803.4 555.4 %reduce-scatter.56.cloned.1.call-start = ((), (), s32[]{:S(2)}) async-start(), calls=%async_computation.42 | async-start | bytes 2433024
  806.9 656.7 %reduce-scatter.54.cloned.1.call-start = ((), (), s32[]{:S(2)}) async-start(), calls=%async_computation.41 | async-start | bytes 2433024
  810.4 757.0 %reduce-scatter.30.cloned.1.call-start = ((), (), s32[]{:S(2)}) async-start(), calls=%async_computation.29 | async-start | bytes 2433024 | tf_op jit(solution)/shard_map/reduce_scatter | solution.py:473
  813.4 26.5 %copy-start.20 = (bf16[192,768]{1,0:T(8,128)(2,1)S(1)}, bf16[192,768]{1,0:T(8,128)(2,1)}, u32[]{:S(2)}) copy-start(bf16[192,768]{1,0:T(8,128)(2,1)} %copy-done.19) | copy-start | bytes 884740
  813.4 26.5 %copy-start.47 = (bf16[192,2048]{1,0:T(8,128)(2,1)S(1)}, bf16[192,2048]{1,0:T(8,128)(2,1)}, u32[]{:S(2)}) copy-start(bf16[192,2048]{1,0:T(8,128)(2,1)} %copy-done.46) | copy-start | bytes 2359300
  813.4 858.7 %reduce-scatter.32.cloned.1.call-start = ((), (), s32[]{:S(2)}) async-start(), calls=%async_computation.30 | async-start | bytes 2433024 | tf_op jit(solution)/shard_map/reduce_scatter | solution.py:474
  839.9 951.7 %reduce-scatter.40.cloned.1.call-start = ((), (), s32[]{:S(2)}) async-start(), calls=%async_computation.34 | async-start | bytes 6488064 | tf_op jit(solution)/shard_map/reduce_scatter | solution.py:482
  843.6 1068.5 %reduce-scatter.42.cloned.1.call-start = ((), (), s32[]{:S(2)}) async-start(), calls=%async_computation.35 | async-start | bytes 6488064 | tf_op jit(solution)/shard_map/reduce_scatter | solution.py:483
  848.5 1183.4 %reduce-scatter.44.cloned.1.call-start = ((), (), s32[]{:S(2)}) async-start(), calls=%async_computation.36 | async-start | bytes 6488064 | tf_op jit(solution)/shard_map/reduce_scatter | solution.py:484
  860.7 43.0 %copy-start.84 = (f32[192]{0:T(256)S(1)}, f32[192]{0:T(256)}, u32[]{:S(2)}) copy-start(f32[192]{0:T(256)} %copy-done.83) | copy-start | bytes 2308
  860.7 43.0 %copy-start.26 = (f32[192,768]{1,0:T(8,128)S(1)}, f32[192,768]{1,0:T(8,128)}, u32[]{:S(2)}) copy-start(f32[192,768]{1,0:T(8,128)} %copy-done.24) | copy-start | bytes 1769476
  (112 other events, 329.5 us)
Sparse Core Ops, SparseCore 0:
  10.9 56.8 all-gather.18
  70.7 53.0 all-gather.14
  126.7 53.0 all-gather.22
  182.6 53.0 all-gather.30
  238.4 53.0 all-gather.26
  293.4 16.3 all-gather.20
  312.0 17.4 all-gather.16
  332.4 54.0 all-gather.24
  389.4 53.0 all-gather.28
  445.2 53.0 all-gather.32
  501.2 57.9 all-gather.34
  562.0 57.8 all-gather.36
  622.8 57.8 all-gather.38
  699.9 22.0 reduce-scatter.51
  724.5 23.2 reduce-scatter.49
  783.9 24.5 reduce-scatter.45
  811.1 25.7 reduce-scatter.47
  842.6 98.9 reduce-scatter.35
  948.3 98.0 reduce-scatter.37
  1052.1 97.9 reduce-scatter.27
  1156.8 98.0 reduce-scatter.33
  1260.8 98.0 reduce-scatter.55
  1365.5 98.0 reduce-scatter.53
  1469.3 98.0 reduce-scatter.29
  1574.0 98.0 reduce-scatter.31
  1678.2 113.3 reduce-scatter.39
  1798.6 113.4 reduce-scatter.41
  1918.3 113.4 reduce-scatter.43
where the time goes:
time: 2040 us
  waiting for transfers between devices  1650 us (81%)
  matrix products  161 us (8%)
  blocking collectives  91.2 us (4%)
  local copies, waits for them, and re-layouts  77.1 us (4%)
  other arithmetic  22.3 us (1%)
    unnamed x34, waiting for transfers between devices  239 us
    reduce_scatter x1, waiting for transfers between devices, per_device(): lax.psum_scatter(up_grad, ('shard', 'ctx'), scatter_dimension=0, tiled=True)  121 us
    reduce_scatter x1, waiting for transfers between devices, per_device(): lax.psum_scatter(down_grad, ('shard', 'ctx'), scatter_dimension=0, tiled=...  120 us
    reduce_scatter x1, waiting for transfers between devices, per_device(): lax.psum_scatter(gate_grad, ('shard', 'ctx'), scatter_dimension=0, tiled=...  119 us
    reduce_scatter x1, waiting for transfers between devices, per_device(): lax.psum_scatter(value_grad, ('shard', 'ctx'), scatter_dimension=0, tiled...  105 us
    reduce_scatter x1, waiting for transfers between devices, per_device(): lax.psum_scatter(self_out_grad, ('shard', 'ctx'), scatter_dimension=0, ti...  105 us
    reduce_scatter x1, waiting for transfers between devices, per_device(): lax.psum_scatter(cross_out_grad, ('shard', 'ctx'), scatter_dimension=0, t...  105 us
    reduce_scatter x1, waiting for transfers between devices, per_device(): lax.psum_scatter(key_grad, ('shard', 'ctx'), scatter_dimension=0, tiled=T...  104 us
  transfers between devices with their start and end apart: 28, of which 23 were waited for; matrix products, arithmetic and copies ran while one was open for 11% of the time, Pallas kernels for 0%

commit v1 on v0

--- a/solution.py
+++ b/solution.py
@@ -212,38 +212,43 @@
     feed_down,
     bias_table,
 ):
-    gathered = (
-        lax.all_gather(gain_self, ("shard", "ctx"), axis=0, tiled=True),
-        lax.all_gather(self_query, ("shard", "ctx"), axis=0, tiled=True),
-        lax.all_gather(self_key, ("shard", "ctx"), axis=0, tiled=True),
-        lax.all_gather(self_value, ("shard", "ctx"), axis=0, tiled=True),
-        lax.all_gather(self_out, ("shard", "ctx"), axis=0, tiled=True),
-        lax.all_gather(gain_cross, ("shard", "ctx"), axis=0, tiled=True),
-        lax.all_gather(cross_query, ("shard", "ctx"), axis=0, tiled=True),
-        lax.all_gather(cross_key, ("shard", "ctx"), axis=0, tiled=True),
-        lax.all_gather(cross_value, ("shard", "ctx"), axis=0, tiled=True),
-        lax.all_gather(cross_out, ("shard", "ctx"), axis=0, tiled=True),
-        lax.all_gather(gain_feed, ("shard", "ctx"), axis=0, tiled=True),
-        lax.all_gather(feed_gate, ("shard", "ctx"), axis=0, tiled=True),
-        lax.all_gather(feed_up, ("shard", "ctx"), axis=0, tiled=True),
-        lax.all_gather(feed_down, ("shard", "ctx"), axis=0, tiled=True),
-    )
+    squares = (
+        self_query,
+        self_key,
+        self_value,
+        self_out,
+        cross_query,
+        cross_key,
+        cross_value,
+        cross_out,
+        feed_gate,
+        feed_up,
+    )
+    gains = jnp.stack((gain_self, gain_cross, gain_feed), axis=1)
+    gains = jnp.pad(gains, ((0, 0), (0, 128 - gains.shape[1])))
+    packed = lax.all_gather(
+        jnp.concatenate(squares + (gains,), axis=1), ("shard", "ctx"), axis=0, tiled=True
+    )
+    whole_feed_down = lax.all_gather(feed_down, ("shard", "ctx"), axis=0, tiled=True)
+    unpacked = []
+    start = 0
+    for part in squares:
+        unpacked.append(lax.slice_in_dim(packed, start, start + part.shape[1], axis=1))
+        start += part.shape[1]
     (
-        whole_gain_self,
         whole_self_query,
         whole_self_key,
         whole_self_value,
         whole_self_out,
-        whole_gain_cross,
         whole_cross_query,
         whole_cross_key,
         whole_cross_value,
         whole_cross_out,
-        whole_gain_feed,
         whole_feed_gate,
         whole_feed_up,
-        whole_feed_down,
-    ) = gathered
+    ) = unpacked
+    gain_rows = lax.slice_in_dim(packed, start, start + 128, axis=1).T
+    whole_gain_self, whole_gain_cross, whole_gain_feed = gain_rows[0], gain_rows[1], gain_rows[2]
     token_rows = inputs.shape[1]
     width = inputs.shape[2]
     head_count = bias_table.shape[1]
@@ -319,54 +324,22 @@
     )
     hidden = gated.astype(jnp.bfloat16)
     outputs = (after_cross + project(hidden, whole_feed_down)).astype(jnp.bfloat16)
-    back_weights = (
-        lax.all_gather(gain_self, ("shard", "ctx"), axis=0, tiled=True),
-        lax.all_gather(self_query, ("shard", "ctx"), axis=0, tiled=True),
-        lax.all_gather(self_key, ("shard", "ctx"), axis=0, tiled=True),
-        lax.all_gather(self_value, ("shard", "ctx"), axis=0, tiled=True),
-        lax.all_gather(self_out, ("shard", "ctx"), axis=0, tiled=True),
-        lax.all_gather(gain_cross, ("shard", "ctx"), axis=0, tiled=True),
-        lax.all_gather(cross_query, ("shard", "ctx"), axis=0, tiled=True),
-        lax.all_gather(cross_key, ("shard", "ctx"), axis=0, tiled=True),
-        lax.all_gather(cross_value, ("shard", "ctx"), axis=0, tiled=True),
-        lax.all_gather(cross_out, ("shard", "ctx"), axis=0, tiled=True),
-        lax.all_gather(gain_feed, ("shard", "ctx"), axis=0, tiled=True),
-        lax.all_gather(feed_gate, ("shard", "ctx"), axis=0, tiled=True),
-        lax.all_gather(feed_up, ("shard", "ctx"), axis=0, tiled=True),
-        lax.all_gather(feed_down, ("shard", "ctx"), axis=0, tiled=True),
-    )
-    (
-        back_gain_self,
-        back_self_query,
-        back_self_key,
-        back_self_value,
-        back_self_out,
-        back_gain_cross,
-        back_cross_query,
-        back_cross_key,
-        back_cross_value,
-        back_cross_out,
-        back_gain_feed,
-        back_feed_gate,
-        back_feed_up,
-        back_feed_down,
-    ) = back_weights
     outer = cotangent[0].astype(jnp.float32)
     grad_feed_out = outer.astype(jnp.bfloat16)
     down_grad = outer_sum(hidden, grad_feed_out)
-    grad_hidden = project_back(grad_feed_out, back_feed_down)
+    grad_hidden = project_back(grad_feed_out, whole_feed_down)
     grad_gate_f, grad_up_f = gated_pull(grad_hidden)
     grad_gate = grad_gate_f.astype(jnp.bfloat16)
     grad_up = grad_up_f.astype(jnp.bfloat16)
     gate_grad = outer_sum(normed_feed, grad_gate)
     up_grad = outer_sum(normed_feed, grad_up)
-    grad_normed_feed = project_back(grad_gate, back_feed_gate) + project_back(grad_up, back_feed_up)
-    _, feed_norm_pull = jax.vjp(normed, after_cross, back_gain_feed.astype(jnp.float32))
+    grad_normed_feed = project_back(grad_gate, whole_feed_gate) + project_back(grad_up, whole_feed_up)
+    _, feed_norm_pull = jax.vjp(normed, after_cross, whole_gain_feed.astype(jnp.float32))
     grad_after_feed, gain_feed_grad = feed_norm_pull(grad_normed_feed)
     grad_after_cross = outer + grad_after_feed
     grad_cross_branch = grad_after_cross.astype(jnp.bfloat16)
     cross_out_grad = outer_sum(cross_att, grad_cross_branch)
-    grad_cross_att = project_back(grad_cross_branch, back_cross_out).astype(jnp.bfloat16)
+    grad_cross_att = project_back(grad_cross_branch, whole_cross_out).astype(jnp.bfloat16)
     grad_cross_heads = split_heads(grad_cross_att, head_count)
     cross_delta = jnp.sum(
         (grad_cross_att.astype(jnp.float32) * cross_exact.reshape(token_rows, width)).reshape(
@@ -412,16 +385,16 @@
     cross_key_grad = outer_sum(encoded_local, grad_cross_k)
     cross_value_grad = outer_sum(encoded_local, grad_cross_v)
     encoder_grad = (
-        project_back(grad_cross_k, back_cross_key) + project_back(grad_cross_v, back_cross_value)
+        project_back(grad_cross_k, whole_cross_key) + project_back(grad_cross_v, whole_cross_value)
     ).astype(jnp.bfloat16)
     cross_query_grad = outer_sum(normed_cross, grad_cross_q)
-    grad_normed_cross = project_back(grad_cross_q, back_cross_query)
-    _, cross_norm_pull = jax.vjp(normed, after_self, back_gain_cross.astype(jnp.float32))
+    grad_normed_cross = project_back(grad_cross_q, whole_cross_query)
+    _, cross_norm_pull = jax.vjp(normed, after_self, whole_gain_cross.astype(jnp.float32))
     grad_after_norm, gain_cross_grad = cross_norm_pull(grad_normed_cross)
     grad_after_self = grad_after_cross + grad_after_norm
     grad_self_branch = grad_after_self.astype(jnp.bfloat16)
     self_out_grad = outer_sum(attended, grad_self_branch)
-    grad_attended = project_back(grad_self_branch, back_self_out).astype(jnp.bfloat16)
+    grad_attended = project_back(grad_self_branch, whole_self_out).astype(jnp.bfloat16)
     grad_heads = split_heads(grad_attended, head_count)
     self_delta = jnp.sum(
         (grad_attended.astype(jnp.float32) * self_exact.reshape(token_rows, width)).reshape(
@@ -460,49 +433,64 @@
     key_grad = outer_sum(normed_self, grad_key)
     value_grad = outer_sum(normed_self, grad_value)
     grad_normed_self = (
-        project_back(grad_query, back_self_query)
-        + project_back(grad_key, back_self_key)
-        + project_back(grad_value, back_self_value)
-    )
-    _, self_norm_pull = jax.vjp(normed, tokens, back_gain_self.astype(jnp.float32))
+        project_back(grad_query, whole_self_query)
+        + project_back(grad_key, whole_self_key)
+        + project_back(grad_value, whole_self_value)
+    )
+    _, self_norm_pull = jax.vjp(normed, tokens, whole_gain_self.astype(jnp.float32))
     grad_tokens_norm, gain_self_grad = self_norm_pull(grad_normed_self)
     input_grad = (grad_after_self + grad_tokens_norm).astype(jnp.bfloat16)
-    reduced = (
-        lax.psum_scatter(gain_self_grad, ("shard", "ctx"), scatter_dimension=0, tiled=True),
-        lax.psum_scatter(query_grad, ("shard", "ctx"), scatter_dimension=0, tiled=True),
-        lax.psum_scatter(key_grad, ("shard", "ctx"), scatter_dimension=0, tiled=True),
-        lax.psum_scatter(value_grad, ("shard", "ctx"), scatter_dimension=0, tiled=True),
-        lax.psum_scatter(self_out_grad, ("shard", "ctx"), scatter_dimension=0, tiled=True),
-        lax.psum_scatter(gain_cross_grad, ("shard", "ctx"), scatter_dimension=0, tiled=True),
-        lax.psum_scatter(cross_query_grad, ("shard", "ctx"), scatter_dimension=0, tiled=True),
-        lax.psum_scatter(cross_key_grad, ("shard", "ctx"), scatter_dimension=0, tiled=True),
-        lax.psum_scatter(cross_value_grad, ("shard", "ctx"), scatter_dimension=0, tiled=True),
-        lax.psum_scatter(cross_out_grad, ("shard", "ctx"), scatter_dimension=0, tiled=True),
-        lax.psum_scatter(gain_feed_grad, ("shard", "ctx"), scatter_dimension=0, tiled=True),
-        lax.psum_scatter(gate_grad, ("shard", "ctx"), scatter_dimension=0, tiled=True),
-        lax.psum_scatter(up_grad, ("shard", "ctx"), scatter_dimension=0, tiled=True),
-        lax.psum_scatter(down_grad, ("shard", "ctx"), scatter_dimension=0, tiled=True),
-    )
-    table_total = lax.psum(table_part, ("shard", "ctx"))
+    square_grads = (
+        query_grad,
+        key_grad,
+        value_grad,
+        self_out_grad,
+        cross_query_grad,
+        cross_key_grad,
+        cross_value_grad,
+        cross_out_grad,
+        gate_grad,
+        up_grad,
+    )
+    packed_grads = jnp.concatenate([g.astype(jnp.bfloat16) for g in square_grads], axis=1)
+    own_packed = lax.psum_scatter(
+        packed_grads, ("shard", "ctx"), scatter_dimension=0, tiled=True
+    ).astype(jnp.float32)
+    own_down = lax.psum_scatter(
+        down_grad.astype(jnp.bfloat16), ("shard", "ctx"), scatter_dimension=0, tiled=True
+    ).astype(jnp.float32)
+    own = []
+    start = 0
+    for part in square_grads:
+        own.append(lax.slice_in_dim(own_packed, start, start + part.shape[1], axis=1))
+        start += part.shape[1]
+    small = lax.psum(
+        (gain_self_grad, gain_cross_grad, gain_feed_grad, table_part), ("shard", "ctx")
+    )
+    slot = lax.axis_index(("shard", "ctx"))
+    own_gains = [
+        lax.dynamic_slice_in_dim(g, slot * gain_self.shape[0], gain_self.shape[0], 0)
+        for g in small[:3]
+    ]
     return (
         outputs[None],
         input_grad[None],
         encoder_grad[None],
-        reduced[0],
-        reduced[1],
-        reduced[2],
-        reduced[3],
-        reduced[4],
-        reduced[5],
-        reduced[6],
-        reduced[7],
-        reduced[8],
-        reduced[9],
-        reduced[10],
-        reduced[11],
-        reduced[12],
-        reduced[13],
-        table_total,
+        own_gains[0],
+        own[0],
+        own[1],
+        own[2],
+        own[3],
+        own_gains[1],
+        own[4],
+        own[5],
+        own[6],
+        own[7],
+        own_gains[2],
+        own[8],
+        own[9],
+        own_down,
+        small[3],
     )
 
 

time: 2040 us -> 754 us (0.37)
  waiting for transfers between devices: 1650 us -> 382 us
  blocking collectives: 91.2 us -> 48.5 us
  local copies, waits for them, and re-layouts: 77.1 us -> 99.5 us
    reduce_scatter x9 -> x2, waiting for transfers between devices: 919 us -> 206 us  [the longest x1 174 us: per_device(): lax.psum_scatter(packed_grads, ('shard', 'ctx'), scatter_dimension=0, til...]
    all_gather x10 -> x1, waiting for transfers between devices: 421 us -> 110 us  [per_device(): lax.all_gather(jnp.concatenate(squares + (gains,), axis=1), ('shard', 'ct...]
    unnamed x34 -> x14, waiting for transfers between devices: 239 us -> 15.1 us
    unnamed x2 -> x0, blocking collectives: 82 us -> none
    psum x0 -> x1, blocking collectives: none -> 39.9 us  [per_device(): lax.psum((gain_self_grad, gain_cross_grad, gain_feed_grad, table_part), (...]
    unnamed x163 -> x195, local copies, waits for them, and re-layouts: 42.2 us -> 49.5 us
  transfers between devices with their start and end apart: 28 -> 10, of which waited for: 23 -> 6; matrix products, arithmetic and copies ran while one was open for 11% -> 24% of each run, Pallas kernels for 0% -> 0%
where the time goes in v1:
time: 754 us; the launch traced here: 743 us
  waiting for transfers between devices  382 us (51%)
  matrix products  153 us (20%)
  local copies, waits for them, and re-layouts  99.5 us (13%)
  blocking collectives  48.5 us (6%)
  other arithmetic  24.6 us (3%)
  loops' own time  18.9 us (3%)
  between operations  15.8 us (2%)
    reduce_scatter x1, waiting for transfers between devices, per_device(): lax.psum_scatter(packed_grads, ('shard', 'ctx'), scatter_dimension=0, til...  174 us
    all_gather x1, waiting for transfers between devices, per_device(): lax.all_gather(jnp.concatenate(squares + (gains,), axis=1), ('shard', 'ct...  110 us
    unnamed x195, local copies, waits for them, and re-layouts  49.5 us
    all_gather x1, waiting for transfers between devices, per_device(): lax.all_gather(feed_down, ('shard', 'ctx'), axis=0, tiled=True)  46.9 us
    psum x1, blocking collectives, per_device(): lax.psum((gain_self_grad, gain_cross_grad, gain_feed_grad, table_part), (...  39.9 us
    reduce_scatter x1, waiting for transfers between devices, per_device(): lax.psum_scatter(down_grad.astype(jnp.bfloat16), ('shard', 'ctx'), scatte...  32.1 us
    dot_general x11, matrix products, project_back(): lax.dot_general(grads, weight, (((1,), (1,)), ((), ())), preferred_elemen...  30 us
    dot_general x11, matrix products, project(): return jnp.dot(left, right, preferred_element_type=jnp.float32)  28 us
  transfers between devices with their start and end apart: 10, of which 6 were waited for; matrix products, arithmetic and copies ran while one was open for 24% of the time, Pallas kernels for 0%

profile of v1, /device:TPU:0, one launch (start us, length us, event | category | flops | bytes accessed | tf_op | source)
XLA Modules:
  0.0 743.0 jit_solution(7741142309615821762)
XLA Ops:
  20.5 110.3 %all-gather.6.cloned.1.call-done = bf16[768,10368]{1,0:T(8,128)(2,1)} async-done(((bf16[24,10368]{1,0:T(8,128)(2,1)}), bf16[768,10368]{1,0:T(8,128)(2,1)}) %all-gather.6.cloned.1.call-update) | async-done | bytes 15925264 | tf_op jit(solution)/shard_map/all_gather | solution.py:229
  132.6 2.4 convolution_convert_fusion.18
  135.3 8.6 %all-gather = bf16[1,512,768]{2,1,0:T(8,128)(2,1)S(1)} all-gather(bf16[1,128,768]{2,1,0:T(8,128)(2,1)S(1)} %copy-done.39), channel_id=2, replica_groups=mesh['shard'=8,'ctx'=4] {'ctx'}, dimensions={1}, use_global_device_ids=true | all-gather | bytes 983040 | tf_op jit(solution)/shard_map/all_gather | solution.py:296
  143.9 46.9 %all-gather.12.cloned.1.call-done = bf16[2048,768]{1,0:T(8,128)(2,1)} async-done(((bf16[64,768]{1,0:T(8,128)(2,1)}), bf16[2048,768]{1,0:T(8,128)(2,1)}) %all-gather.12.cloned.1.call-update) | async-done | bytes 3145744 | tf_op jit(solution)/shard_map/all_gather | solution.py:232
  190.9 4.2 fusion.112
  197.0 2.5 convolution_convert_fusion.19
  199.6 3.0 convolution_convert_fusion.11
  202.5 3.0 convolution_convert_fusion.12
  205.6 3.8 all-gather.10.cloned.1.call-done
  210.9 26.2 %while.43 = (s32[]{:T(128)}, f32[12,192]{1,0:T(8,128)S(1)}, f32[12,192]{1,0:T(8,128)S(1)}, s32[192]{0:T(256)S(1)}, s32[3]{0:T(128)S(1)}, /*index=5*/s32[768]{0:T...) while((s32[]{:T(128)}, f32[12,192]{1,0:T(8,128)S(1)}, ...), condition=%wide.region_8.9_spmd.clone, body=%wide.region_4.8_spmd.clone.sunk | while | flops 311782656 | bytes 11923778 | solution.py:94
  237.2 2.4 copy.129
  239.5 31.5 %while.44 = (s32[]{:T(128)}, f32[192,12,64]{0,2,1:T(8,128)S(1)}, f32[192,12,64]{0,2,1:T(8,128)S(1)}, s32[3]{0:T(128)S(1)}, bf16[768,768]{0,1:T(8,128)(2,1)}, /*i...) while((s32[]{:T(128)}, f32[192,12,64]{0,2,1:T(8,128)S(1)}, ...), condition=%wide.region_11.12_spmd.clone, body=%wide.region_9.11_spmd.clone.sunk | while | flops 465125376 | bytes 18104656 | solution.py:133
  274.7 2.4 convolution_convert_fusion.16
  287.7 2.8 fusion.40
  290.5 4.7 fusion.55
  295.2 3.6 fusion.38
  298.9 3.9 multiply_reduce_fusion.1
  303.9 2.5 convert_multiply_fusion.2
  308.7 4.3 convolution_convert_fusion.13
  314.2 4.3 multiply_convert_fusion
  318.6 2.4 copy.156
  321.0 3.2 multiply_convert_fusion.2
  325.3 2.4 copy.154
  327.7 2.9 fusion.59
  330.6 2.7 multiply_reduce_fusion.2
  334.3 2.7 convert_multiply_fusion.1
  337.1 2.3 copy.137
  341.8 43.0 %while.45 = (s32[]{:T(128)}, f32[192,12,64]{0,2,1:T(8,128)S(1)}, f32[32,12]{0,1:T(8,128)S(1)}, f32[3,256,12,64]{1,3,2,0:T(8,128)}, bf16[3,256,12,64]{1,3,2,0:T(8...) while((s32[]{:T(128)}, f32[192,12,64]{0,2,1:T(8,128)S(1)}, ...), condition=%wide.region_22.23_spmd.clone, body=%wide.region_20.22_spmd.clone.sunk | while | flops 657703680 | bytes 33845680 | solution.py:190
  386.8 3.8 copy.158
  390.6 4.9 reshape.319
  395.6 3.8 copy.159
  399.4 4.9 reshape.321
  404.4 2.8 convolution_convert_fusion
  409.8 2.4 copy.146
  421.9 2.5 fusion.57
  425.9 2.4 fusion.56
  428.3 2.4 copy.147
  430.7 2.5 convolution_convert_fusion.5
  433.3 2.4 copy.143
  435.7 14.2 %reduce-scatter.21.cloned.1.call-done = bf16[192,768]{1,0:T(8,128)(2,1)} async-done(((bf16[768,768]{1,0:T(8,128)(2,1)}), bf16[192,768]{1,0:T(8,128)(2,1)}) %reduce-scatter.21.cloned.1.call-update) | async-done | bytes 294928
  449.9 2.5 convolution_convert_fusion.4
  452.4 2.5 copy.144
  463.7 2.8 fusion.36
  466.5 2.8 fusion.35
  475.7 2.6 fusion.66
  482.2 39.9 %all-reduce.1 = (f32[768]{0:T(1024)S(1)}, f32[768]{0:T(1024)S(1)}, f32[768]{0:T(1024)S(1)}, f32[32,12]{0,1:T(8,128)}) all-reduce(f32[768]{0:T(1024)S(1)} %get-tuple-element.506, f32[768]{0:T(1024)S(1)} %copy-done.76, f32[768]{0:T(1024)S(1)} %copy-done.75, f32[32,12]{0,1:T(8,128)S(1)} %copy-done.74), channel_id=1, replica_groups=mesh['shard'=8,'ctx'=4] {'shard','ctx'}, use_global_device_ids=true, to_apply=%region_29.30 | all-reduce | flops 2688 | bytes 21504 | tf_op jit(solution)/shard_map/psum | solution.py:467
  524.8 32.1 %reduce-scatter.17.cloned.1.call-done = bf16[64,768]{1,0:T(8,128)(2,1)} async-done(((bf16[2048,768]{1,0:T(8,128)(2,1)}), bf16[64,768]{1,0:T(8,128)(2,1)}) %reduce-scatter.17.cloned.1.call-update) | async-done | bytes 98320 | tf_op jit(solution)/shard_map/reduce_scatter | solution.py:459
  558.5 173.8 %reduce-scatter.15.cloned.1.call-done = bf16[24,10240]{1,0:T(8,128)(2,1)} async-done(((bf16[768,10240]{1,0:T(8,128)(2,1)}), bf16[24,10240]{1,0:T(8,128)(2,1)}) %reduce-scatter.15.cloned.1.call-update) | async-done | bytes 491536 | tf_op jit(solution)/shard_map/reduce_scatter | solution.py:456
  (401 shorter events, 166.3 us)
Async XLA Ops:
  7.2 125.4 %copy-start.8 = (bf16[1,192,768]{2,1,0:T(8,128)(2,1)S(1)}, bf16[1,192,768]{2,1,0:T(8,128)(2,1)}, u32[]{:S(2)}) copy-start(bf16[1,192,768]{2,1,0:T(8,128)(2,1)} %param.26) | copy-start | bytes 884740
  7.2 123.5 %all-gather.6.cloned.1.call-start = ((), (), s32[]{:S(2)}) async-start(), calls=%async_computation.6 | async-start | bytes 16422912 | tf_op jit(solution)/shard_map/all_gather | solution.py:229
  16.1 119.1 %copy-start.79 = (s32[8]{0:T(128)S(1)}, s32[8]{0:T(128)}, u32[]{:S(2)}) copy-start(s32[8]{0:T(128)} %param.29) | copy-start | bytes 100
  16.1 119.3 %copy-start.39 = (bf16[1,128,768]{2,1,0:T(8,128)(2,1)S(1)}, bf16[1,128,768]{2,1,0:T(8,128)(2,1)}, u32[]{:S(2)}) copy-start(bf16[1,128,768]{2,1,0:T(8,128)(2,1)} %param.27) | copy-start | bytes 589828
  16.9 174.0 %all-gather.12.cloned.1.call-start = ((), (), s32[]{:S(2)}) async-start(), calls=%async_computation.9 | async-start | bytes 3244032 | tf_op jit(solution)/shard_map/all_gather | solution.py:232
  17.6 191.7 %all-gather.10.cloned.1.call-start = ((), (), s32[]{:S(2)}) async-start(), calls=%async_computation.8 | async-start | bytes 1474560 | tf_op jit(solution)/shard_map/all_gather | solution.py:272
  20.4 114.7 %copy-start.70 = (f32[192]{0:T(256)}, f32[192]{0:T(256)S(1)}, u32[]{:S(2)}) copy-start(f32[192]{0:T(256)S(1)} %fusion.100) | copy-start | bytes 2308
  20.4 170.4 %copy-start.31 = (bf16[1,192,768]{2,1,0:T(8,128)(2,1)S(1)}, bf16[1,192,768]{2,1,0:T(8,128)(2,1)}, u32[]{:S(2)}) copy-start(bf16[1,192,768]{2,1,0:T(8,128)(2,1)} %param.28) | copy-start | bytes 884740
  20.5 176.5 %copy-start.66 = (f32[192]{0:T(256)}, f32[192]{0:T(256)S(1)}, u32[]{:S(2)}) copy-start(f32[192]{0:T(256)S(1)} %fusion.133) | copy-start | bytes 2308
  132.6 64.4 %copy-start.60 = (f32[768]{0:T(1024)}, f32[768]{0:T(1024)S(1)}, u32[]{:S(2)}) copy-start(f32[768]{0:T(1024)S(1)} %get-tuple-element.510) | copy-start | bytes 9220
  135.0 102.1 %all-gather.8.cloned.1.call-start = ((), (), s32[]{:S(2)}) async-start(), calls=%async_computation.7 | async-start | bytes 1474560 | tf_op jit(solution)/shard_map/all_gather | solution.py:273
  199.5 222.3 %reduce-scatter.25.cloned.1.call-start = ((), (), s32[]{:S(2)}) async-start(), calls=%async_computation.15 | async-start | bytes 983040
  202.5 8.4 %copy-start.36 = (f32[32,12]{0,1:T(8,128)S(1)}, f32[32,12]{0,1:T(8,128)}, u32[]{:S(2)}) copy-start(f32[32,12]{0,1:T(8,128)} %param.45) | copy-start | bytes 4612
  274.1 8.4 %copy-start.15 = (f32[192,768]{1,0:T(8,128)}, f32[192,768]{1,0:T(8,128)S(1)}, u32[]{:S(2)}) copy-start(f32[192,768]{1,0:T(8,128)S(1)} %get-tuple-element.613) | copy-start | bytes 1769476
  274.1 4.2 copy-start.29
  279.2 5.3 copy-start
  282.5 3.9 copy-start.25
  284.5 18.3 %copy-start.3 = (f32[192,768]{1,0:T(8,128)}, f32[192,768]{1,0:T(8,128)S(1)}, u32[]{:S(2)}) copy-start(f32[192,768]{1,0:T(8,128)S(1)} %get-tuple-element.619) | copy-start | bytes 1769476
  298.9 3.9 copy-start.32
  308.7 5.6 copy-start.12
  321.0 104.9 %reduce-scatter.23.cloned.1.call-start = ((), (), s32[]{:S(2)}) async-start(), calls=%async_computation.14 | async-start | bytes 983040
  325.3 5.3 copy-start.16
  325.3 5.3 copy-start.64
  325.3 5.3 copy-start.69
  330.6 3.7 copy-start.35
  337.0 4.8 copy-start.1
  337.0 4.8 copy-start.38
  337.0 4.8 copy-start.51
  337.0 4.8 copy-start.59
  337.1 4.8 copy-start.72
  337.1 4.8 copy-start.81
  341.7 89.0 %reduce-scatter.19.cloned.1.call-start = ((), (), s32[]{:S(2)}) async-start(), calls=%async_computation.12 | async-start | bytes 1474560
  384.9 5.8 copy-start.73
  390.6 4.9 copy-start.48
  395.5 54.4 %reduce-scatter.21.cloned.1.call-start = ((), (), s32[]{:S(2)}) async-start(), calls=%async_computation.13 | async-start | bytes 1474560
  399.4 5.0 copy-start.13
  399.4 5.0 copy-start.33
  404.3 152.6 %reduce-scatter.17.cloned.1.call-start = ((), (), s32[]{:S(2)}) async-start(), calls=%async_computation.11 | async-start | bytes 3244032 | tf_op jit(solution)/shard_map/reduce_scatter | solution.py:459
  407.2 5.0 copy-start.26
  407.2 325.2 %reduce-scatter.15.cloned.1.call-start = ((), (), s32[]{:S(2)}) async-start(), calls=%async_computation.10 | async-start | bytes 16220160 | tf_op jit(solution)/shard_map/reduce_scatter | solution.py:456
  473.8 4.5 copy-start.49
  475.7 4.5 copy-start.10
  475.7 4.5 copy-start.57
  478.3 3.9 copy-start.74
  478.3 3.9 copy-start.75
  478.3 4.0 copy-start.76
  478.3 45.6 %copy-start.71 = (f32[192]{0:T(256)S(1)}, f32[192]{0:T(256)}, u32[]{:S(2)}) copy-start(f32[192]{0:T(256)} %copy-done.70) | copy-start | bytes 2308
  478.3 45.6 %copy-start.7 = (f32[192,768]{1,0:T(8,128)S(1)}, f32[192,768]{1,0:T(8,128)}, u32[]{:S(2)}) copy-start(f32[192,768]{1,0:T(8,128)} %copy-done.5) | copy-start | bytes 1769476
  (52 other events, 105.9 us)
Sparse Core Ops, SparseCore 0:
  17.0 113.6 all-gather.5
  133.6 57.2 all-gather.11
  193.0 16.3 all-gather.9
  211.4 17.4 all-gather.7
  321.1 23.2 reduce-scatter.24
  346.9 23.2 reduce-scatter.22
  395.6 25.7 reduce-scatter.18
  424.1 25.6 reduce-scatter.20
  455.3 101.5 reduce-scatter.16
  562.8 169.5 reduce-scatter.14

commit v2 on v1

v2 whole, which is shorter than its diff:
```python
import functools

import jax
import jax.numpy as jnp
from jax import lax
from jax.experimental import pallas as pl
from jax.experimental.pallas import tpu as pltpu
from jax.sharding import PartitionSpec as P

EPSILON = 1e-06
MASKED = -1e30
PRECISE = lax.Precision.HIGHEST
LANES = 128
BOTH = ("shard", "ctx")
F32 = jnp.float32
BF16 = jnp.bfloat16


def inverse_norm(values):
    return lax.rsqrt(jnp.mean(values * values, axis=-1, keepdims=True) + EPSILON)


def norm_back(values, inverse, gain, grads):
    weighted = gain * grads
    middle = jnp.mean(weighted * values, axis=-1, keepdims=True)
    return inverse * weighted - values * (inverse * inverse * inverse) * middle


def project(left, right):
    return jnp.dot(left, right, preferred_element_type=F32)


def project_back(grads, weight):
    return lax.dot_general(grads, weight, (((1,), (1,)), ((), ())), preferred_element_type=F32)


def outer_sum(left, grads):
    return lax.dot_general(left, grads, (((0,), (0,)), ((), ())), preferred_element_type=F32)


def swap(values, mask):
    count = lax.axis_size("shard") * lax.axis_size("ctx")
    return lax.ppermute(values, BOTH, [(i, i ^ mask) for i in range(count)])


def pick(values, index, axis):
    return lax.dynamic_index_in_dim(values, index, axis, keepdims=False)


def paired(first, second, flag):
    joined = jnp.concatenate((first, second), axis=0)
    return jnp.where(flag == 0, joined, jnp.concatenate((second, first), axis=0))


def ctx_gather(values, quads):
    if not quads:
        return lax.all_gather(values, "ctx", axis=0, tiled=True)
    slot = lax.axis_index("ctx")
    far = swap(values, 2)
    near = paired(values, swap(values, 1), slot % 2)
    far = paired(far, swap(far, 1), slot % 2)
    return paired(near, far, slot // 2)


def ctx_scatter_sum(values, quads):
    if not quads:
        return lax.psum_scatter(values, "ctx", scatter_dimension=0, tiled=True).astype(F32)
    slot = lax.axis_index("ctx")
    core, row = slot % 2, slot // 2
    parts = values.reshape(2, 2, values.shape[0] // 4, values.shape[1])
    summed = pick(parts, core, 1).astype(F32) + swap(pick(parts, 1 - core, 1), 1).astype(F32)
    summed = summed.astype(BF16)
    return pick(summed, row, 0).astype(F32) + swap(pick(summed, 1 - row, 0), 2).astype(F32)


def scatter_sum(values, quads):
    if not quads:
        return lax.psum_scatter(values, BOTH, scatter_dimension=0, tiled=True).astype(F32)
    shard, ctx = lax.axis_index("shard"), lax.axis_index("ctx")
    core, row, column, layer = ctx % 2, ctx // 2, shard % 2, shard // 2
    layers = lax.axis_size("shard") // 2
    rows = values.shape[0] // (layers * 8)
    half = values.shape[1] // 2 // LANES * LANES
    parts = values.reshape(layers, 2, 2, 2, rows, values.shape[1])
    chip = pick(parts, core, 3).astype(F32) + swap(pick(parts, 1 - core, 3), 1).astype(F32)
    chip = chip.astype(BF16)
    left, right = chip[..., :half], chip[..., half:]
    left_in, right_in = swap(pick(left, 1 - column, 1), 4), swap(pick(right, 1 - row, 2), 2)
    left = (pick(left, column, 1).astype(F32) + left_in.astype(F32)).astype(BF16)
    right = (pick(right, row, 2).astype(F32) + right_in.astype(F32)).astype(BF16)
    left_in, right_in = swap(pick(left, 1 - row, 1), 2), swap(pick(right, 1 - column, 1), 4)
    left = pick(left, row, 1).astype(F32) + left_in.astype(F32)
    right = pick(right, column, 1).astype(F32) + right_in.astype(F32)
    plane = jnp.concatenate((left, right), axis=-1).astype(BF16)
    total = pick(plane, layer, 0).astype(F32)
    for step in range(1, layers):
        total = total + swap(pick(plane, layer ^ step, 0), 8 * step).astype(F32)
    return total


def small_sum(values, quads):
    if not quads:
        return lax.psum(values, BOTH)
    for mask in (1, 2, 4):
        values = values + swap(values, mask)
    arrived = [swap(values, 8 * step) for step in range(1, lax.axis_size("shard") // 2)]
    layer = lax.axis_index("shard") // 2
    stacked = jnp.stack([values] + arrived)
    return sum(pick(stacked, layer ^ step, 0) for step in range(stacked.shape[0]))


def fold(values, rows, columns):
    lead = values.shape[:-2]
    tall, wide = values.shape[-2] // 8, rows // 8
    step = values.shape[-1] // wide
    cut = values.reshape(lead + (tall, 8, values.shape[-1]))
    bands = []
    for band in range(wide):
        bands.append(
            jnp.concatenate(
                [cut[..., t, :, band * step : (band + 1) * step] for t in range(tall)], axis=-1
            )
        )
    return jnp.concatenate(bands, axis=-2)


def unfold(values, rows, columns):
    tall, wide = rows // 8, values.shape[-2] // 8
    step = columns // wide
    out = []
    for t in range(tall):
        out.append(
            jnp.concatenate(
                [
                    values[..., w * 8 : (w + 1) * 8, t * step : (t + 1) * step]
                    for w in range(wide)
                ],
                axis=-1,
            )
        )
    return jnp.concatenate(out, axis=-2)


def head_mask(shape, head_size, head):
    lane = lax.broadcasted_iota(jnp.int32, shape, 1)
    return lane // head_size == head


def pad_keys(source, target, span_rows):
    spans = source.shape[0] // span_rows
    for b in range(spans):
        target[b * LANES : b * LANES + span_rows, :] = source[
            b * span_rows : (b + 1) * span_rows, :
        ]


def skew(values, right):
    width = values.shape[1]
    row = lax.broadcasted_iota(jnp.int32, values.shape, 0)
    for bit in range((values.shape[0] - 1).bit_length()):
        shift = 1 << bit
        moved = pltpu.roll(values, shift if right else width - shift, 1)
        values = jnp.where((row >> bit) & 1 == 1, moved, values)
    return values


def dot_rows(left, right):
    return lax.dot_general(left, right, (((1,), (1,)), ((), ())), preferred_element_type=F32)


def dot_columns(left, right):
    return lax.dot_general(left, right, (((0,), (0,)), ((), ())), preferred_element_type=F32)


def probabilities(scores):
    top = jnp.max(scores, axis=1, keepdims=True)
    raised = jnp.exp(scores - top)
    return raised * (1.0 / jnp.sum(raised, axis=1, keepdims=True))


def self_forward_kernel(
    kind_ref, q_ref, k_ref, v_ref, line_ref, p_ref, o_ref, kp, vp, tables, s_ref, *, span_rows, head_size
):
    @pl.when(pl.program_id(0) == 0)
    def _():
        kp[...] = jnp.zeros(kp.shape, kp.dtype)
        vp[...] = jnp.zeros(vp.shape, vp.dtype)

    pad_keys(k_ref, kp, span_rows)
    pad_keys(v_ref, vp, span_rows)
    pair = LANES // head_size
    spans = k_ref.shape[0] // span_rows
    query_spans = q_ref.shape[0] // span_rows
    inside = lax.broadcasted_iota(jnp.int32, (span_rows, LANES), 1) < span_rows
    out = jnp.zeros(o_ref.shape, F32)
    for h in range(pair):
        tables[0] = jnp.full((span_rows, LANES), MASKED, F32)
        for k in range(4):
            line = jnp.broadcast_to(
                line_ref[0, h * 4 + k : h * 4 + k + 1, :], (span_rows, 2 * LANES)
            )
            if k < 3:
                line = skew(line, True)
            tables[k + 1] = jnp.where(inside, line[:, :LANES], MASKED)
        q = jnp.where(head_mask(q_ref.shape, head_size, h), q_ref[...], jnp.zeros((), BF16))
        s_ref[...] = dot_rows(q, kp[...]) * (head_size**-0.5)
        for a in range(query_spans):
            for b in range(spans):
                rows, columns = pl.ds(a * span_rows, span_rows), pl.ds(b * LANES, LANES)
                s_ref[rows, columns] = s_ref[rows, columns] + tables[kind_ref[a * spans + b]]
        probs = probabilities(s_ref[...]).astype(BF16)
        p_ref[h] = probs
        v = jnp.where(head_mask(vp.shape, head_size, h), vp[...], jnp.zeros((), BF16))
        out = out + jnp.dot(probs, v, preferred_element_type=F32)
    o_ref[...] = out.astype(BF16)


def cross_forward_kernel(q_ref, k_ref, v_ref, p_ref, o_ref, *, head_size):
    out = jnp.zeros(o_ref.shape, F32)
    for h in range(LANES // head_size):
        q = jnp.where(head_mask(q_ref.shape, head_size, h), q_ref[...], jnp.zeros((), BF16))
        probs = probabilities(dot_rows(q, k_ref[...]) * (head_size**-0.5)).astype(BF16)
        p_ref[h] = probs
        v = jnp.where(head_mask(v_ref.shape, head_size, h), v_ref[...], jnp.zeros((), BF16))
        out = out + jnp.dot(probs, v, preferred_element_type=F32)
    o_ref[...] = out.astype(BF16)


def pair_backward(h, q_ref, do_ref, keys, values, p_ref, head_size):
    grads = jnp.where(head_mask(do_ref.shape, head_size, h), do_ref[...], jnp.zeros((), BF16))
    q = jnp.where(head_mask(q_ref.shape, head_size, h), q_ref[...], jnp.zeros((), BF16))
    probs_low = p_ref[h]
    probs = probs_low.astype(F32)
    grad_probs = dot_rows(grads, values)
    delta = jnp.sum(probs * grad_probs, axis=1, keepdims=True)
    grad_scores = (probs * (grad_probs - delta)).astype(BF16)
    k = jnp.where(head_mask(keys.shape, head_size, h), keys, jnp.zeros((), BF16))
    grad_q = jnp.dot(grad_scores, k, preferred_element_type=F32)
    return grad_scores, grad_q, dot_columns(grad_scores, q), dot_columns(probs_low, grads)


def self_backward_kernel(
    kind_ref,
    q_ref,
    do_ref,
    k_ref,
    v_ref,
    p_ref,
    dq_ref,
    dk_ref,
    dv_ref,
    line_ref,
    kp,
    vp,
    tables,
    s_ref,
    *,
    span_rows,
    head_size,
):
    @pl.when(pl.program_id(0) == 0)
    def _():
        kp[...] = jnp.zeros(kp.shape, kp.dtype)
        vp[...] = jnp.zeros(vp.shape, vp.dtype)

    pad_keys(k_ref, kp, span_rows)
    pad_keys(v_ref, vp, span_rows)
    pair = LANES // head_size
    spans = k_ref.shape[0] // span_rows
    query_spans = q_ref.shape[0] // span_rows
    scale = head_size**-0.5
    grad_q = jnp.zeros(dq_ref.shape, F32)
    grad_k = jnp.zeros(kp.shape, F32)
    grad_v = jnp.zeros(vp.shape, F32)
    blank = jnp.zeros((span_rows, LANES), F32)
    for h in range(pair):
        scores, part_q, part_k, part_v = pair_backward(
            h, q_ref, do_ref, kp[...], vp[...], p_ref, head_size
        )
        grad_q, grad_k, grad_v = grad_q + part_q, grad_k + part_k, grad_v + part_v
        s_ref[...] = scores.astype(F32)
        tables[...] = jnp.zeros(tables.shape, F32)
        for a in range(query_spans):
            for b in range(spans):
                kind = kind_ref[a * spans + b]
                rows, columns = pl.ds(a * span_rows, span_rows), pl.ds(b * LANES, LANES)
                tables[kind] = tables[kind] + s_ref[rows, columns]
        for k in range(4):
            block = jnp.concatenate((tables[k + 1], blank), axis=1)
            if k < 3:
                block = skew(block, False)
            line_ref[0, h * 4 + k : h * 4 + k + 1, :] = jnp.sum(block, axis=0, keepdims=True)
    dq_ref[...] = (grad_q * scale).astype(BF16)
    grad_k = (grad_k * scale).astype(BF16)
    grad_v = grad_v.astype(BF16)
    for b in range(spans):
        dk_ref[b * span_rows : (b + 1) * span_rows, :] = grad_k[b * LANES : b * LANES + span_rows]
        dv_ref[b * span_rows : (b + 1) * span_rows, :] = grad_v[b * LANES : b * LANES + span_rows]


def cross_backward_kernel(
    q_ref, do_ref, k_ref, v_ref, p_ref, dq_ref, dk_ref, dv_ref, *, head_size
):
    scale = head_size**-0.5
    grad_q = jnp.zeros(dq_ref.shape, F32)
    grad_k = jnp.zeros(dk_ref.shape, F32)
    grad_v = jnp.zeros(dv_ref.shape, F32)
    for h in range(LANES // head_size):
        _, part_q, part_k, part_v = pair_backward(
            h, q_ref, do_ref, k_ref[...], v_ref[...], p_ref, head_size
        )
        grad_q, grad_k, grad_v = grad_q + part_q, grad_k + part_k, grad_v + part_v
    dq_ref[...] = (grad_q * scale).astype(BF16)
    dk_ref[...] = (grad_k * scale).astype(BF16)
    dv_ref[...] = grad_v.astype(BF16)


PARAMS = pltpu.CompilerParams(vmem_limit_bytes=48 * 1024 * 1024)


def columns_of(rows, offset=0):
    return pl.BlockSpec((rows, LANES), lambda g, *_: (0, g + offset))


def probs_spec(pair, rows, keys):
    return pl.BlockSpec((pair, rows, keys), lambda g, *_: (g, 0, 0))


def lines_spec():
    return pl.BlockSpec((1, 8, 2 * LANES), lambda g, *_: (g, 0, 0))


def self_forward(kinds, queries, keys_values, lines, span_rows, head_size):
    rows, width = queries.shape
    key_rows = keys_values.shape[0]
    groups, pair = width // LANES, LANES // head_size
    padded = key_rows // span_rows * LANES
    return pl.pallas_call(
        functools.partial(self_forward_kernel, span_rows=span_rows, head_size=head_size),
        grid_spec=pltpu.PrefetchScalarGridSpec(
            num_scalar_prefetch=1,
            grid=(groups,),
            in_specs=[
                columns_of(rows),
                columns_of(key_rows),
                columns_of(key_rows, groups),
                lines_spec(),
            ],
            out_specs=[probs_spec(pair, rows, padded), columns_of(rows)],
            scratch_shapes=[
                pltpu.VMEM((padded, LANES), BF16),
                pltpu.VMEM((padded, LANES), BF16),
                pltpu.VMEM((5, span_rows, LANES), F32),
                pltpu.VMEM((rows, padded), F32),
            ],
        ),
        out_shape=[
            jax.ShapeDtypeStruct((groups * pair, rows, padded), BF16),
            jax.ShapeDtypeStruct((rows, width), BF16),
        ],
        compiler_params=PARAMS,
    )(kinds, queries, keys_values, keys_values, lines)


def self_backward(kinds, queries, grads, keys_values, probs, span_rows, head_size):
    rows, width = queries.shape
    key_rows = keys_values.shape[0]
    groups, pair = width // LANES, LANES // head_size
    padded = probs.shape[2]
    return pl.pallas_call(
        functools.partial(self_backward_kernel, span_rows=span_rows, head_size=head_size),
        grid_spec=pltpu.PrefetchScalarGridSpec(
            num_scalar_prefetch=1,
            grid=(groups,),
            in_specs=[
                columns_of(rows),
                columns_of(rows),
                columns_of(key_rows),
                columns_of(key_rows, groups),
                probs_spec(pair, rows, padded),
            ],
            out_specs=[
                columns_of(rows),
                columns_of(key_rows),
                columns_of(key_rows),
                lines_spec(),
            ],
            scratch_shapes=[
                pltpu.VMEM((padded, LANES), BF16),
                pltpu.VMEM((padded, LANES), BF16),
                pltpu.VMEM((5, span_rows, LANES), F32),
                pltpu.VMEM((rows, padded), F32),
            ],
        ),
        out_shape=[
            jax.ShapeDtypeStruct((rows, width), BF16),
            jax.ShapeDtypeStruct((key_rows, width), BF16),
            jax.ShapeDtypeStruct((key_rows, width), BF16),
            jax.ShapeDtypeStruct((groups, 8, 2 * LANES), F32),
        ],
        compiler_params=PARAMS,
    )(kinds, queries, grads, keys_values, keys_values, probs)


def cross_forward(queries, keys_values, head_size):
    rows, width = queries.shape
    key_rows = keys_values.shape[0]
    groups, pair = width // LANES, LANES // head_size
    return pl.pallas_call(
        functools.partial(cross_forward_kernel, head_size=head_size),
        grid=(groups,),
        in_specs=[columns_of(rows), columns_of(key_rows), columns_of(key_rows, groups)],
        out_specs=[probs_spec(pair, rows, key_rows), columns_of(rows)],
        out_shape=[
            jax.ShapeDtypeStruct((groups * pair, rows, key_rows), BF16),
            jax.ShapeDtypeStruct((rows, width), BF16),
        ],
        compiler_params=PARAMS,
    )(queries, keys_values, keys_values)


def cross_backward(queries, grads, keys_values, probs, head_size):
    rows, width = queries.shape
    key_rows = keys_values.shape[0]
    groups, pair = width // LANES, LANES // head_size
    return pl.pallas_call(
        functools.partial(cross_backward_kernel, head_size=head_size),
        grid=(groups,),
        in_specs=[
            columns_of(rows),
            columns_of(rows),
            columns_of(key_rows),
            columns_of(key_rows, groups),
            probs_spec(pair, rows, key_rows),
        ],
        out_specs=[columns_of(rows), columns_of(key_rows), columns_of(key_rows)],
        out_shape=[
            jax.ShapeDtypeStruct((rows, width), BF16),
            jax.ShapeDtypeStruct((key_rows, width), BF16),
            jax.ShapeDtypeStruct((key_rows, width), BF16),
        ],
        compiler_params=PARAMS,
    )(queries, grads, keys_values, keys_values, probs)


def line_buckets(buckets, span_rows, table_rows):
    place = jnp.arange(2 * LANES, dtype=jnp.int32)
    place = jnp.where(place < LANES, place, place - 2 * LANES)
    distance = jnp.arange(3, dtype=jnp.int32)[:, None] * span_rows - place[None, :]
    known = buckets.shape[0]
    hits = distance[:, :, None] == jnp.arange(known, dtype=jnp.int32)
    bucket = jnp.sum(jnp.where(hits, buckets, 0), axis=-1)
    bucket = jnp.where(distance >= known, table_rows - 1, bucket)
    onehot = bucket[:, :, None] == jnp.arange(table_rows, dtype=jnp.int32)
    return (onehot & (distance >= 0)[:, :, None]).astype(F32), distance >= 0


def bias_lines(table, onehot, valid, pair):
    heads = table.shape[1]
    lines = jnp.einsum("kmb,bh->hkm", onehot, table, precision=PRECISE)
    lines = jnp.where(valid[None], lines, MASKED)
    last = jnp.broadcast_to(table[-1][:, None, None], (heads, 1, lines.shape[2]))
    lines = jnp.concatenate((lines, last), axis=1)
    return lines.reshape(heads // pair, pair * 4, lines.shape[2])


def table_gradient(lines, onehot, heads):
    lines = lines.reshape(heads, 4, lines.shape[2])
    grads = jnp.einsum("hkm,kmb->bh", lines[:, :3], onehot, precision=PRECISE)
    return grads.at[-1].add(jnp.sum(lines[:, 3], axis=-1))


def block_kinds(span_order, first_span, query_spans):
    own = lax.dynamic_slice_in_dim(span_order, first_span, query_spans, 0)
    apart = own[:, None] - span_order[None, :]
    kinds = jnp.where(apart < 0, 0, jnp.where(apart > 2, 4, apart + 1))
    return kinds.reshape(-1).astype(jnp.int32)


def per_device(
    inputs,
    encoder_states,
    cotangent,
    span_order,
    buckets,
    gain_self,
    self_query,
    self_key,
    self_value,
    self_out,
    gain_cross,
    cross_query,
    cross_key,
    cross_value,
    cross_out,
    gain_feed,
    feed_gate,
    feed_up,
    feed_down,
    bias_table,
):
    shards, slots = lax.axis_size("shard"), lax.axis_size("ctx")
    shard_rows, width = self_query.shape
    down_rows = feed_down.shape[0]
    feed = feed_gate.shape[1]
    quads = slots == 4 and shards in (2, 4, 8) and shard_rows % 8 == 0 and down_rows % 8 == 0
    token_rows = inputs.shape[1]
    heads = bias_table.shape[1]
    head_size = width // heads
    pair = LANES // head_size
    table_rows = bias_table.shape[0]
    span_rows = token_rows // 2
    slot = lax.axis_index("ctx")
    enc_rows = encoder_states.shape[1]

    gains = jnp.stack((gain_self, gain_cross, gain_feed), axis=1)
    gains = jnp.pad(gains, ((0, 0), (0, LANES - gains.shape[1])))
    mine = [
        self_query,
        self_key,
        self_value,
        self_out,
        cross_query,
        cross_key,
        cross_value,
        cross_out,
        feed_gate,
        feed_up,
        gains,
    ]
    if quads:
        mine.append(fold(feed_down, shard_rows, feed_down.size // shard_rows))
    packed = lax.all_gather(jnp.concatenate(mine, axis=1), BOTH, axis=0, tiled=True)

    def columns(first, last):
        return lax.slice_in_dim(packed, first, last, axis=1)

    w_query, w_key_value = columns(0, width), columns(width, 3 * width)
    w_out, w_cross_query = columns(3 * width, 4 * width), columns(4 * width, 5 * width)
    w_cross_key_value, w_cross_out = columns(5 * width, 7 * width), columns(7 * width, 8 * width)
    base = 8 * width
    w_gate, w_up = columns(base, base + feed), columns(base + feed, base + 2 * feed)
    base = base + 2 * feed
    gain_rows = columns(base, base + LANES).T.astype(F32)
    g_self, g_cross, g_feed = gain_rows[0], gain_rows[1], gain_rows[2]
    if quads:
        folded = columns(base + LANES, packed.shape[1])
        folded = folded.reshape(shards * slots, shard_rows, folded.shape[1])
        w_down = unfold(folded, down_rows, width).reshape(feed, width)
    else:
        w_down = lax.all_gather(feed_down, BOTH, axis=0, tiled=True)

    sequence = ctx_gather(jnp.concatenate((inputs[0], encoder_states[0]), axis=0), quads)
    sequence = sequence.reshape(slots, token_rows + enc_rows, width)
    tokens_all = sequence[:, :token_rows].reshape(slots * token_rows, width).astype(F32)
    encoded = sequence[:, token_rows:].reshape(slots * enc_rows, width)

    onehot, valid = line_buckets(buckets, span_rows, table_rows)
    lines = bias_lines(bias_table, onehot, valid, pair)
    kinds = block_kinds(span_order, slot * 2, 2)

    tokens = inputs[0].astype(F32)
    unit_all = tokens_all * inverse_norm(tokens_all)
    normed_all = (unit_all * g_self).astype(BF16)
    inverse_self = inverse_norm(tokens)
    unit_self = tokens * inverse_self
    normed_self = (unit_self * g_self).astype(BF16)
    queries = project(normed_self, w_query).astype(BF16)
    keys_values = project(normed_all, w_key_value).astype(BF16)
    probs, attended = self_forward(kinds, queries, keys_values, lines, span_rows, head_size)
    after_self = tokens + project(attended, w_out)
    inverse_cross = inverse_norm(after_self)
    unit_cross = after_self * inverse_cross
    normed_cross = (unit_cross * g_cross).astype(BF16)
    cross_q = project(normed_cross, w_cross_query).astype(BF16)
    cross_kv = project(encoded, w_cross_key_value).astype(BF16)
    cross_probs, cross_att = cross_forward(cross_q, cross_kv, head_size)
    after_cross = after_self + project(cross_att, w_cross_out)
    inverse_feed = inverse_norm(after_cross)
    unit_feed = after_cross * inverse_feed
    normed_feed = (unit_feed * g_feed).astype(BF16)
    gate_pre = project(normed_feed, w_gate)
    up_pre = project(normed_feed, w_up)
    gated, gated_pull = jax.vjp(
        lambda first, second: jax.nn.gelu(first, approximate=True) * second, gate_pre, up_pre
    )
    hidden = gated.astype(BF16)
    outputs = (after_cross + project(hidden, w_down)).astype(BF16)

    grad_out = cotangent[0]
    outer = grad_out.astype(F32)
    grad_gate, grad_up = gated_pull(project_back(grad_out, w_down))
    grad_gate, grad_up = grad_gate.astype(BF16), grad_up.astype(BF16)
    down_grad = outer_sum(hidden, grad_out).astype(BF16)
    feed_grads = [
        outer_sum(normed_feed, grad_gate).astype(BF16),
        outer_sum(normed_feed, grad_up).astype(BF16),
    ]
    if quads:
        folded = down_grad.reshape(shards * slots, down_rows, width)
        folded = fold(folded, shard_rows, down_rows * width // shard_rows)
        feed_grads.append(folded.reshape(shards * slots * shard_rows, folded.shape[2]))
    own_feed = scatter_sum(jnp.concatenate(feed_grads, axis=1), quads)
    own_gate, own_up = own_feed[:, :feed], own_feed[:, feed : 2 * feed]
    if quads:
        own_down = unfold(own_feed[:, 2 * feed :], down_rows, width)
    else:
        own_down = scatter_sum(down_grad, quads)
    grad_normed = project_back(grad_gate, w_gate) + project_back(grad_up, w_up)
    gain_feed_grad = jnp.sum(grad_normed * unit_feed, axis=0)
    grad_cross_out = outer + norm_back(after_cross, inverse_feed, g_feed, grad_normed)

    grad_low = grad_cross_out.astype(BF16)
    cross_out_grad = outer_sum(cross_att, grad_low).astype(BF16)
    grad_att = project_back(grad_low, w_cross_out).astype(BF16)
    grad_cq, part_ck, part_cv = cross_backward(cross_q, grad_att, cross_kv, cross_probs, head_size)
    cross_query_grad = outer_sum(normed_cross, grad_cq).astype(BF16)
    part_ckv = jnp.concatenate((part_ck, part_cv), axis=1)
    cross_kv_grad = outer_sum(encoded, part_ckv).astype(BF16)
    encoder_grad = ctx_scatter_sum(project_back(part_ckv, w_cross_key_value).astype(BF16), quads)
    grad_normed = project_back(grad_cq, w_cross_query)
    gain_cross_grad = jnp.sum(grad_normed * unit_cross, axis=0)
    grad_self_out = grad_cross_out + norm_back(after_self, inverse_cross, g_cross, grad_normed)

    grad_low = grad_self_out.astype(BF16)
    self_out_grad = outer_sum(attended, grad_low).astype(BF16)
    grad_att = project_back(grad_low, w_out).astype(BF16)
    grad_q, part_k, part_v, grad_lines = self_backward(
        kinds, queries, grad_att, keys_values, probs, span_rows, head_size
    )
    query_grad = outer_sum(normed_self, grad_q).astype(BF16)
    part_kv = jnp.concatenate((part_k, part_v), axis=1)
    kv_grad = outer_sum(normed_all, part_kv).astype(BF16)
    own = scatter_sum(
        jnp.concatenate(
            (query_grad, kv_grad, self_out_grad, cross_query_grad, cross_kv_grad, cross_out_grad),
            axis=1,
        ),
        quads,
    )
    own = [own[:, i * width : (i + 1) * width] for i in range(8)]
    grad_kv_normed = project_back(part_kv, w_key_value)
    grad_q_normed = project_back(grad_q, w_query)
    gain_self_grad = jnp.sum(grad_kv_normed * unit_all, axis=0) + jnp.sum(
        grad_q_normed * unit_self, axis=0
    )
    grad_normed = grad_q_normed + ctx_scatter_sum(grad_kv_normed.astype(BF16), quads)
    input_grad = grad_self_out + norm_back(tokens, inverse_self, g_self, grad_normed)

    table_part = table_gradient(grad_lines, onehot, heads)
    small = jnp.concatenate(
        (gain_self_grad, gain_cross_grad, gain_feed_grad, table_part.reshape(-1))
    )
    tile = 8 * LANES
    extent = small.shape[0]
    small = jnp.pad(small, (0, -extent % tile)).reshape(-1, LANES)
    small = small_sum(small, quads).reshape(-1)
    position = lax.axis_index(BOTH) * shard_rows
    own_gains = [
        lax.dynamic_slice_in_dim(small, i * width + position, shard_rows, 0) for i in range(3)
    ]
    table_total = small[3 * width : extent].reshape(table_rows, heads)
    return (
        outputs[None],
        input_grad.astype(BF16)[None],
        encoder_grad.astype(BF16)[None],
        own_gains[0],
        own[0],
        own[1],
        own[2],
        own[3],
        own_gains[1],
        own[4],
        own[5],
        own[6],
        own[7],
        own_gains[2],
        own_gate,
        own_up,
        own_down,
        table_total,
    )


def solution(mesh):
    in_specs = (
        P("shard", "ctx", None),
        P("shard", "ctx", None),
        P("shard", "ctx", None),
        P(),
        P(),
        P(("shard", "ctx")),
        P(("shard", "ctx"), None),
        P(("shard", "ctx"), None),
        P(("shard", "ctx"), None),
        P(("shard", "ctx"), None),
        P(("shard", "ctx")),
        P(("shard", "ctx"), None),
        P(("shard", "ctx"), None),
        P(("shard", "ctx"), None),
        P(("shard", "ctx"), None),
        P(("shard", "ctx")),
        P(("shard", "ctx"), None),
        P(("shard", "ctx"), None),
        P(("shard", "ctx"), None),
        P(),
    )
    out_specs = (
        P("shard", "ctx", None),
        P("shard", "ctx", None),
        P("shard", "ctx", None),
        P(("shard", "ctx")),
        P(("shard", "ctx"), None),
        P(("shard", "ctx"), None),
        P(("shard", "ctx"), None),
        P(("shard", "ctx"), None),
        P(("shard", "ctx")),
        P(("shard", "ctx"), None),
        P(("shard", "ctx"), None),
        P(("shard", "ctx"), None),
        P(("shard", "ctx"), None),
        P(("shard", "ctx")),
        P(("shard", "ctx"), None),
        P(("shard", "ctx"), None),
        P(("shard", "ctx"), None),
        P(),
    )
    return jax.shard_map(
        per_device, mesh=mesh, in_specs=in_specs, out_specs=out_specs, check_vma=False
    )
```

time: 754 us -> 493 us (0.65)
  waiting for transfers between devices: 382 us -> 220 us
  matrix products: 153 us -> 70 us
  blocking collectives: 48.5 us -> 0 us
  Pallas kernels: 0 us -> 47.9 us
  local copies, waits for them, and re-layouts: 99.5 us -> 52.3 us
  starting transfers between devices: 0.66 us -> 45.1 us
  loops' own time: 18.9 us -> 0 us
  other arithmetic: 24.6 us -> 32.7 us
    reduce_scatter x2 -> x0, waiting for transfers between devices: 206 us -> none  [the longest x1 174 us: per_device(): lax.psum_scatter(packed_grads, ('shard', 'ctx'), scatter_dimension=0, til...]
    ppermute x0 -> x29, waiting for transfers between devices: none -> 112 us  [swap(): return lax.ppermute(values, BOTH, [(i, i ^ mask) for i in range(count)])]
    dot_general x57 -> x11, matrix products: 99.7 us -> 23.6 us  [the longest x9 23.3 us: project(): return jnp.dot(left, right, preferred_element_type=F32)]
    all_gather x4 -> x1, waiting for transfers between devices: 161 us -> 108 us  [per_device(): lax.all_gather(jnp.concatenate(mine, axis=1), BOTH, axis=0, tiled=True)]
    pallas_call x0 -> x4, Pallas kernels: none -> 47.9 us  [the longest x1 20.8 us: self_backward(): pl.pallas_call(functools.partial(self_backward_kernel, span_rows=span_row...]
    ppermute x0 -> x29, starting transfers between devices: none -> 45.1 us  [swap(): return lax.ppermute(values, BOTH, [(i, i ^ mask) for i in range(count)])]
    psum x1 -> x0, blocking collectives: 39.9 us -> none  [per_device(): lax.psum((gain_self_grad, gain_cross_grad, gain_feed_grad, table_part), (...]
    unnamed x195 -> x120, local copies, waits for them, and re-layouts: 49.5 us -> 20.1 us
  transfers between devices with their start and end apart: 10 -> 30, of which waited for: 6 -> 16; matrix products, arithmetic and copies ran while one was open for 24% -> 14% of each run, Pallas kernels for 0% -> 0%
where the time goes in v2:
time: 493 us; the launch traced here: 484 us
  waiting for transfers between devices  220 us (45%)
  matrix products  70 us (14%)
  local copies, waits for them, and re-layouts  52.3 us (11%)
  Pallas kernels  47.9 us (10%)
  starting transfers between devices  45.1 us (9%)
  other arithmetic  32.7 us (7%)
  between operations  15.9 us (3%)
    ppermute x29, waiting for transfers between devices, swap(): return lax.ppermute(values, BOTH, [(i, i ^ mask) for i in range(count)])  112 us
    all_gather x1, waiting for transfers between devices, per_device(): lax.all_gather(jnp.concatenate(mine, axis=1), BOTH, axis=0, tiled=True)  108 us
    ppermute x29, starting transfers between devices, swap(): return lax.ppermute(values, BOTH, [(i, i ^ mask) for i in range(count)])  45.1 us
    dot_general x9, matrix products, project_back(): lax.dot_general(grads, weight, (((1,), (1,)), ((), ())), preferred_elemen...  23.7 us
    dot_general x9, matrix products, project(): return jnp.dot(left, right, preferred_element_type=F32)  23.3 us
    dot_general x9, matrix products, outer_sum(): lax.dot_general(left, grads, (((0,), (0,)), ((), ())), preferred_element_...  22.7 us
    pallas_call x1, Pallas kernels, self_backward(): pl.pallas_call(functools.partial(self_backward_kernel, span_rows=span_row...  20.8 us
    unnamed x120, local copies, waits for them, and re-layouts  20.1 us
  transfers between devices with their start and end apart: 30, of which 16 were waited for; matrix products, arithmetic and copies ran while one was open for 14% of the time, Pallas kernels for 0%

profile of v2, /device:TPU:0, one launch (start us, length us, event | category | flops | bytes accessed | tf_op | source)
XLA Modules:
  0.0 484.0 jit_solution(2584788717286464178)
XLA Ops:
  23.9 3.0 collective-permute-start.1
  28.3 12.4 %collective-permute-done.1 = bf16[320,768]{1,0:T(8,128)(2,1)S(1)} collective-permute-done((bf16[320,768]{1,0:T(8,128)(2,1)S(1)}, bf16[320,768]{1,0:T(8,128)(2,1)S(1)}, u32[]{:S(2)}, u32[]{:S(2)}) %collective-permute-start.1) | collective-permute-done | bytes 491552 | tf_op jit(solution)/shard_map/ppermute | solution.py:43
  44.2 107.8 %all-gather.2.cloned.1.call-done = bf16[768,12416]{1,0:T(8,128)(2,1)} async-done(((bf16[24,12416]{1,0:T(8,128)(2,1)}), bf16[768,12416]{1,0:T(8,128)(2,1)}) %all-gather.2.cloned.1.call-update) | async-done | bytes 19070992 | tf_op jit(solution)/shard_map/all_gather | solution.py:533
  152.0 2.3 slice.599
  158.0 2.2 convolution_convert_fusion.14.q_ref
  160.2 3.6 convolution_convert_fusion.2.k_ref.v_ref
  163.8 14.5 %shard_map.331 = (bf16[12,192,1024]{2,1,0:T(8,128)(2,1)}, bf16[192,768]{1,0:T(8,128)(2,1)S(1)}) custom-call(s32[16]{0:T(128)S(1)} %select_n.191.kind_ref, bf16[192,768]{1,0:T(8,128)(2,1)S(1)} %convolution_convert_fusion.14.q_ref, bf16[768,1536]{1,0:T(8,128)(2,1)S(1)} %convolution_convert_fusion.2.k_ref.v_ref, ...), custom_call_target="tpu_custom_call" | custom-call | tf_op jit(solution)/shard_map/pallas_call | solution.py:338
  180.2 3.3 convolution_convert_fusion.6.k_ref.v_ref
  185.3 4.9 %shard_map.332 = (bf16[12,192,512]{2,1,0:T(8,128)(2,1)S(1)}, bf16[192,768]{1,0:T(8,128)(2,1)S(1)}) custom-call(bf16[192,768]{1,0:T(8,128)(2,1)S(1)} %convolution_convert_fusion.13.q_ref, bf16[512,1536]{1,0:T(8,128)(2,1)S(1)} %convolution_convert_fusion.6.k_ref.v_ref, bf16[512,1536]{1,0:T(8,128)(2,1)S(1)} %convolution_convert_fusion.6.k_ref.v_ref), custom_call_target="tpu_custom_call" | custom-call | tf_op jit(solution)/shard_map/pallas_call | solution.py:409
  190.2 2.7 multiply_reduce_fusion.6
  195.3 2.7 fusion.6
  198.0 3.8 fusion.28
  203.3 2.7 convolution_convert_fusion.3
  206.0 2.7 convolution_convert_fusion.4
  208.7 2.6 convolution_convert_fusion.5
  211.4 3.1 fusion.4
  214.5 3.2 multiply_reduce_fusion.2
  220.0 7.7 %shard_map.333 = (bf16[192,768]{1,0:T(8,128)(2,1)S(1)}, bf16[512,768]{1,0:T(8,128)(2,1)S(1)}, bf16[512,768]{1,0:T(8,128)(2,1)S(1)}) custom-call(bf16[192,768]{1,0:T(8,128)(2,1)S(1)} %convolution_convert_fusion.13.q_ref, bf16[192,768]{1,0:T(8,128)(2,1)S(1)} %convolution_convert_fusion.12.do_ref, bf16[512,1536]{1,0:T(8,128)(2,1)S(1)} %convolution_convert_fusion.6.k_ref.v_ref, ...), custom_call_target="tpu_custom_call" | custom-call | tf_op jit(solution)/shard_map/pallas_call | solution.py:426
  227.7 2.0 multiply_reduce_fusion.3
  230.0 2.0 convolution_convert_fusion.11.do_ref
  232.0 20.8 %shard_map.334 = (bf16[192,768]{1,0:T(8,128)(2,1)S(1)}, bf16[768,768]{1,0:T(8,128)(2,1)S(1)}, bf16[768,768]{1,0:T(8,128)(2,1)S(1)}, f32[6,8,256]{2,1,0:T(8,128)S(1)}) custom-call(s32[16]{0:T(128)S(1)} %select_n.191.kind_ref, bf16[192,768]{1,0:T(8,128)(2,1)S(1)} %convolution_convert_fusion.14.q_ref, bf16[192,768]{1,0:T(8,128)(2,1)S(1)} %convolution_convert_fusion.11.do_ref, ...), custom_call_target="tpu_custom_call" | custom-call | tf_op jit(solution)/shard_map/pallas_call | solution.py:370
  255.7 2.4 copy.123
  258.1 3.0 constant_dynamic-update-slice_fusion.36
  261.1 4.4 multiply_reduce_fusion
  266.9 3.7 fusion.32
  272.0 5.3 %fusion.3 = bf16[768,6144]{1,0:T(8,128)(2,1)} fusion(bf16[768,6144]{1,0:T(8,128)(2,1)} %get-tuple-element.239, bf16[768,768]{1,0:T(8,128)(2,1)S(1)} %copy-done.20, bf16[768,1536]{1,0:T(8,128)(2,1)} %get-tuple-element.238), kind=kOutput, calls=%fused_computation.11 | convolution fusion | flops 1813118976 | bytes 5898240 | tf_op jit(solution)/shard_map/dot_general | solution.py:38
  280.5 2.9 fusion.2
  285.0 7.0 %constant_dynamic-slice_fusion.3 = (bf16[4,2,2,1,24,6144]{5,4,3,2,1,0:T(8,128)(2,1)}, bf16[4,2,2,1,24,6144]{5,4,3,2,1,0:T(8,128)(2,1)S(1)}) fusion(bf16[4,2,2,2,24,6144]{5,4,3,2,1,0:T(8,128)(2,1)} %bitcast.469, s32[]{:T(128)S(6)} %select_n.205, s32[]{:T(128)S(6)} %select_n.206), kind=kLoop, calls=%fused_computation.322 | loop fusion | bytes 18874376 | tf_op jit(solution)/shard_map/jit(dynamic_index_in_dim)/dynamic_slice | solution.py:47
  292.1 2.7 copy.197
  295.4 2.1 pad_maximum_fusion.1
  297.8 4.5 pad_maximum_fusion
  302.3 2.6 dynamic-slice_bitcast_fusion
  304.9 2.4 copy-done.5
  311.9 5.9 %collective-permute-done.4 = bf16[192,768]{1,0:T(8,128)(2,1)S(1)} collective-permute-done((bf16[192,768]{1,0:T(8,128)(2,1)S(1)}, bf16[192,768]{1,0:T(8,128)(2,1)S(1)}, u32[]{:S(2)}, u32[]{:S(2)}) %collective-permute-start.4) | collective-permute-done | bytes 294944 | tf_op jit(solution)/shard_map/ppermute | solution.py:43
  322.6 4.8 collective-permute-done.6
  329.7 2.3 collective-permute-done.9
  333.5 2.8 collective-permute-start.10
  339.5 5.7 %fusion.1 = bf16[4,2,2,24,6144]{4,3,0,1,2:T(8,128)(2,1)S(1)} fusion(bf16[4,2,2,24,6144]{4,3,0,1,2:T(8,128)(2,1)} %collective-permute-done.13, bf16[4,2,2,1,24,6144]{5,4,3,2,1,0:T(8,128)(2,1)} %get-tuple-element.97), kind=kLoop, calls=%fused_computation.4 | loop fusion | flops 9437184 | bytes 14155776 | tf_op jit(solution)/shard_map/convert_element_type | solution.py:86
  350.0 4.1 fusion
  357.1 18.9 %collective-permute-done.14 = bf16[4,2,24,3072]{3,2,0,1:T(8,128)(2,1)} collective-permute-done((bf16[4,2,24,3072]{3,2,0,1:T(8,128)(2,1)}, bf16[4,2,24,3072]{3,2,0,1:T(8,128)(2,1)}, u32[]{:S(2)}, u32[]{:S(2)}) %collective-permute-start.14) | collective-permute-done | bytes 1179680 | tf_op jit(solution)/shard_map/ppermute | solution.py:43
  381.6 19.6 %collective-permute-done.22 = bf16[4,2,24,3072]{3,2,0,1:T(8,128)(2,1)S(1)} collective-permute-done((bf16[4,2,24,3072]{3,2,0,1:T(8,128)(2,1)S(1)}, bf16[4,2,24,3072]{3,2,0,1:T(8,128)(2,1)S(1)}, u32[]{:S(2)}, u32[]{:S(2)}) %collective-permute-start.22) | collective-permute-done | bytes 1179680 | tf_op jit(solution)/shard_map/ppermute | solution.py:43
  404.9 19.8 %collective-permute-done.23 = bf16[4,24,3072]{2,1,0:T(8,128)(2,1)S(1)} collective-permute-done((bf16[4,24,3072]{2,1,0:T(8,128)(2,1)S(1)}, bf16[4,24,3072]{2,1,0:T(8,128)(2,1)S(1)}, u32[]{:S(2)}, u32[]{:S(2)}) %collective-permute-start.23) | collective-permute-done | bytes 589856 | tf_op jit(solution)/shard_map/ppermute | solution.py:43
  425.1 2.4 collective-permute-start.28
  430.0 2.4 collective-permute-start.20
  432.4 4.6 collective-permute-done.28
  436.9 15.8 %collective-permute-start.18 = (bf16[24,6144]{1,0:T(8,128)(2,1)S(1)}, bf16[24,6144]{1,0:T(8,128)(2,1)S(1)}, u32[]{:S(2)}, u32[]{:S(2)}) collective-permute-start(bf16[24,6144]{1,0:T(8,128)(2,1)S(1)} %get-tuple-element.160), channel_id=1, source_target_pairs={{0,8},{1,9},{2,10},{3,11},{4,12},{5,13},{6,14},{7,15},{8,0},{9,1},... | collective-permute-start | bytes 884744 | tf_op jit(solution)/shard_map/ppermute | solution.py:43
  452.7 10.8 %collective-permute-done.27 = bf16[24,6144]{1,0:T(8,128)(2,1)S(1)} collective-permute-done((bf16[24,6144]{1,0:T(8,128)(2,1)S(1)}, bf16[24,6144]{1,0:T(8,128)(2,1)S(1)}, u32[]{:S(2)}, u32[]{:S(2)}) %collective-permute-start.27) | collective-permute-done | bytes 294944 | tf_op jit(solution)/shard_map/ppermute | solution.py:43
  464.5 10.5 %collective-permute-done.19 = bf16[24,6144]{1,0:T(8,128)(2,1)S(1)} collective-permute-done((bf16[24,6144]{1,0:T(8,128)(2,1)S(1)}, bf16[24,6144]{1,0:T(8,128)(2,1)S(1)}, u32[]{:S(2)}, u32[]{:S(2)}) %collective-permute-start.19) | collective-permute-done | bytes 294944 | tf_op jit(solution)/shard_map/ppermute | solution.py:43
  (288 shorter events, 84.8 us)
Async XLA Ops:
  7.2 33.7 %copy-start.27 = (bf16[1,128,768]{2,1,0:T(8,128)(2,1)S(1)}, bf16[1,128,768]{2,1,0:T(8,128)(2,1)}, u32[]{:S(2)}) copy-start(bf16[1,128,768]{2,1,0:T(8,128)(2,1)} %param.23) | copy-start | bytes 589828
  7.2 33.5 %copy-start.13 = (bf16[1,192,768]{2,1,0:T(8,128)(2,1)S(1)}, bf16[1,192,768]{2,1,0:T(8,128)(2,1)}, u32[]{:S(2)}) copy-start(bf16[1,192,768]{2,1,0:T(8,128)(2,1)} %param.22) | copy-start | bytes 884740
  7.2 19.7 %copy-start.41 = (s32[8]{0:T(128)S(1)}, s32[8]{0:T(128)}, u32[]{:S(2)}) copy-start(s32[8]{0:T(128)} %param.25) | copy-start | bytes 100
  7.2 19.8 %copy-start.40 = (s32[128]{0:T(128)S(1)}, s32[128]{0:T(128)}, u32[]{:S(2)}) copy-start(s32[128]{0:T(128)} %param.26) | copy-start | bytes 1540
  7.2 20.4 %copy-start.38 = (f32[32,12]{0,1:T(8,128)S(1)}, f32[32,12]{0,1:T(8,128)}, u32[]{:S(2)}) copy-start(f32[32,12]{0,1:T(8,128)} %param.41) | copy-start | bytes 4612
  7.2 144.8 %all-gather.2.cloned.1.call-start = ((), (), s32[]{:S(2)}) async-start(), calls=%async_computation | async-start | bytes 19666944 | tf_op jit(solution)/shard_map/all_gather | solution.py:533
  23.9 16.9 %collective-permute-start.1 = (bf16[320,768]{1,0:T(8,128)(2,1)S(1)}, bf16[320,768]{1,0:T(8,128)(2,1)S(1)}, u32[]{:S(2)}, u32[]{:S(2)}) collective-permute-start(bf16[320,768]{1,0:T(8,128)(2,1)S(1)} %pad_maximum_fusion.2), channel_id=1, source_target_pairs={{0,2},{1,3},{2,0},{3,1},{4,6},{5,7},{6,4},{7,5},{8,10},{9,11},{10,... | collective-permute-start | bytes 1474568 | tf_op jit(solution)/shard_map/ppermute | solution.py:43
  26.9 14.0 %collective-permute-start = (bf16[320,768]{1,0:T(8,128)(2,1)S(1)}, bf16[320,768]{1,0:T(8,128)(2,1)S(1)}, u32[]{:S(2)}, u32[]{:S(2)}) collective-permute-start(bf16[320,768]{1,0:T(8,128)(2,1)S(1)} %pad_maximum_fusion.2), channel_id=1, source_target_pairs={{0,1},{1,0},{2,3},{3,2},{4,5},{5,4},{6,7},{7,6},{8,9},{9,8},{10,11... | collective-permute-start | bytes 1474568 | tf_op jit(solution)/shard_map/ppermute | solution.py:43
  40.7 1.9 collective-permute-start.2
  43.8 113.9 %copy-start.7 = (bf16[1280,768]{1,0:T(8,128)(2,1)}, bf16[1280,768]{1,0:T(8,128)(2,1)S(1)}, u32[]{:S(2)}) copy-start(bf16[1280,768]{1,0:T(8,128)(2,1)S(1)} %maximum_select_fusion) | copy-start | bytes 5898244
  43.8 136.4 %copy-start.23 = (bf16[4,128,768]{2,1,0:T(8,128)(2,1)}, bf16[4,128,768]{2,1,0:T(8,128)(2,1)S(1)}, u32[]{:S(2)}) copy-start(bf16[4,128,768]{2,1,0:T(8,128)(2,1)S(1)} %slice.593) | copy-start | bytes 2359300
  158.0 5.8 %copy-start.19 = (bf16[768,768]{1,0:T(8,128)(2,1)}, bf16[768,768]{1,0:T(8,128)(2,1)S(1)}, u32[]{:S(2)}) copy-start(bf16[768,768]{1,0:T(8,128)(2,1)S(1)} %multiply_convert_fusion) | copy-start | bytes 3538948
  180.2 49.6 %copy-start.17 = (f32[192,768]{1,0:T(8,128)}, f32[192,768]{1,0:T(8,128)S(1)}, u32[]{:S(2)}) copy-start(f32[192,768]{1,0:T(8,128)S(1)} %get-tuple-element.231) | copy-start | bytes 1769476
  185.2 7.7 %copy-start.33 = (bf16[32,8,256]{2,1,0:T(8,128)(2,1)S(1)}, bf16[32,8,256]{2,1,0:T(8,128)(2,1)}, u32[]{:S(2)}) copy-start(bf16[32,8,256]{2,1,0:T(8,128)(2,1)} %get-tuple-element.150) | copy-start | bytes 393220
  185.2 7.7 %copy-start.34 = (bf16[32,8,256]{2,1,0:T(8,128)(2,1)S(1)}, bf16[32,8,256]{2,1,0:T(8,128)(2,1)}, u32[]{:S(2)}) copy-start(bf16[32,8,256]{2,1,0:T(8,128)(2,1)} %get-tuple-element.151) | copy-start | bytes 393220
  185.2 7.7 %copy-start.35 = (bf16[32,8,256]{2,1,0:T(8,128)(2,1)S(1)}, bf16[32,8,256]{2,1,0:T(8,128)(2,1)}, u32[]{:S(2)}) copy-start(bf16[32,8,256]{2,1,0:T(8,128)(2,1)} %get-tuple-element.152) | copy-start | bytes 393220
  217.9 11.8 %copy-start.11 = (f32[192,768]{1,0:T(8,128)}, f32[192,768]{1,0:T(8,128)S(1)}, u32[]{:S(2)}) copy-start(f32[192,768]{1,0:T(8,128)S(1)} %subtract_add_fusion.1) | copy-start | bytes 1769476
  266.5 40.8 %collective-permute-start.3 = (bf16[2,192,768]{2,1,0:T(8,128)(2,1)}, bf16[2,192,768]{2,1,0:T(8,128)(2,1)}, u32[]{:S(2)}, u32[]{:S(2)}) collective-permute-start(bf16[2,192,768]{2,1,0:T(8,128)(2,1)} %dynamic-slice_bitcast_fusion.8), channel_id=1, source_target_pairs={{0,1},{1,0},{2,3},{3,2},{4,5},{5,4},{6,7},{7,6},{8,9},{9,8},{10,11... | collective-permute-start | bytes 1769480 | tf_op jit(solution)/shard_map/ppermute | solution.py:43
  271.5 39.3 %collective-permute-start.5 = (bf16[2,128,768]{2,1,0:T(8,128)(2,1)}, bf16[2,128,768]{2,1,0:T(8,128)(2,1)}, u32[]{:S(2)}, u32[]{:S(2)}) collective-permute-start(bf16[2,128,768]{2,1,0:T(8,128)(2,1)} %dynamic-slice_bitcast_fusion.9), channel_id=1, source_target_pairs={{0,1},{1,0},{2,3},{3,2},{4,5},{5,4},{6,7},{7,6},{8,9},{9,8},{10,11... | collective-permute-start | bytes 1179656 | tf_op jit(solution)/shard_map/ppermute | solution.py:43
  271.9 6.9 %copy-start.4 = (bf16[192,768]{1,0:T(8,128)(2,1)S(1)}, bf16[192,768]{1,0:T(8,128)(2,1)}, u32[]{:S(2)}) copy-start(bf16[192,768]{1,0:T(8,128)(2,1)} %copy-done.3) | copy-start | bytes 884740
  271.9 6.9 %copy-start.18 = (f32[192,768]{1,0:T(8,128)S(1)}, f32[192,768]{1,0:T(8,128)}, u32[]{:S(2)}) copy-start(f32[192,768]{1,0:T(8,128)} %copy-done.17) | copy-start | bytes 1769476
  294.7 44.8 %collective-permute-start.13 = (bf16[4,2,2,24,6144]{4,3,0,1,2:T(8,128)(2,1)}, bf16[4,2,2,24,6144]{4,3,0,1,2:T(8,128)(2,1)}, u32[]{:S(2)}, u32[]{:S(2)}) collective-permute-start(bf16[4,2,2,24,6144]{4,3,0,1,2:T(8,128)(2,1)} %bitcast.444), channel_id=1, source_target_pairs={{0,1},{1,0},{2,3},{3,2},{4,5},{5,4},{6,7},{7,6},{8,9},{9,8},{10,11... | collective-permute-start | bytes 14155784 | tf_op jit(solution)/shard_map/ppermute | solution.py:43
  307.2 10.6 %copy-start.15 = (bf16[1,192,768]{2,1,0:T(8,128)(2,1)S(1)}, bf16[1,192,768]{2,1,0:T(8,128)(2,1)}, u32[]{:S(2)}) copy-start(bf16[1,192,768]{2,1,0:T(8,128)(2,1)} %param.22) | copy-start | bytes 884740
  308.6 9.2 %collective-permute-start.4 = (bf16[192,768]{1,0:T(8,128)(2,1)S(1)}, bf16[192,768]{1,0:T(8,128)(2,1)S(1)}, u32[]{:S(2)}, u32[]{:S(2)}) collective-permute-start(bf16[192,768]{1,0:T(8,128)(2,1)S(1)} %dynamic-slice_bitcast_fusion.10), channel_id=1, source_target_pairs={{0,2},{1,3},{2,0},{3,1},{4,6},{5,7},{6,4},{7,5},{8,10},{9,11},{10,... | collective-permute-start | bytes 884744 | tf_op jit(solution)/shard_map/ppermute | solution.py:43
  310.7 39.2 %collective-permute-start.21 = (bf16[4,2,2,24,6144]{4,3,2,1,0:T(8,128)(2,1)}, bf16[4,2,2,24,6144]{4,3,2,1,0:T(8,128)(2,1)}, u32[]{:S(2)}, u32[]{:S(2)}) collective-permute-start(bf16[4,2,2,24,6144]{4,3,2,1,0:T(8,128)(2,1)} %dynamic-slice_bitcast_fusion), channel_id=1, source_target_pairs={{0,1},{1,0},{2,3},{3,2},{4,5},{5,4},{6,7},{7,6},{8,9},{9,8},{10,11... | collective-permute-start | bytes 14155784 | tf_op jit(solution)/shard_map/ppermute | solution.py:43
  319.8 1.6 collective-permute-start.7
  319.9 7.5 %collective-permute-start.6 = (bf16[128,768]{1,0:T(8,128)(2,1)S(1)}, bf16[128,768]{1,0:T(8,128)(2,1)S(1)}, u32[]{:S(2)}, u32[]{:S(2)}) collective-permute-start(bf16[128,768]{1,0:T(8,128)(2,1)S(1)} %dynamic-slice_bitcast_fusion.11), channel_id=1, source_target_pairs={{0,2},{1,3},{2,0},{3,1},{4,6},{5,7},{6,4},{7,5},{8,10},{9,11},{10,... | collective-permute-start | bytes 589832 | tf_op jit(solution)/shard_map/ppermute | solution.py:43
  321.5 6.7 %collective-permute-start.8 = (f32[24,128]{1,0:T(8,128)S(1)}, f32[24,128]{1,0:T(8,128)S(1)}, u32[]{:S(2)}, u32[]{:S(2)}) collective-permute-start(f32[24,128]{1,0:T(8,128)S(1)} %fusion.150), channel_id=1, source_target_pairs={{0,2},{1,3},{2,0},{3,1},{4,6},{5,7},{6,4},{7,5},{8,10},{9,11},{10,... | collective-permute-start | bytes 36872 | tf_op jit(solution)/shard_map/ppermute | solution.py:43
  328.2 3.8 collective-permute-start.9
  331.9 5.5 %collective-permute-start.12 = (f32[24,128]{1,0:T(8,128)S(1)}, f32[24,128]{1,0:T(8,128)S(1)}, u32[]{:S(2)}, u32[]{:S(2)}) collective-permute-start(f32[24,128]{1,0:T(8,128)S(1)} %add.326), channel_id=1, source_target_pairs={{0,24},{1,25},{2,26},{3,27},{4,28},{5,29},{6,30},{7,31},{8,16},{9,... | collective-permute-start | bytes 36872 | tf_op jit(solution)/shard_map/ppermute | solution.py:43
  333.4 4.6 collective-permute-start.11
  333.5 4.5 collective-permute-start.10
  339.5 10.5 %slice-start = ((s8[9437184]{0:T(1024)(128)(4,1)}), s8[4194304]{0:T(1024)(128)(4,1)S(1)}, s32[]{:S(2)}) async-start(s8[9437184]{0:T(1024)(128)(4,1)} %bitcast.447), calls=%async_computation.1 | async-start | bytes 8388608
  339.5 10.5 %slice-start.1 = ((s8[9437184]{0:T(1024)(128)(4,1)}), s8[4194304]{0:T(1024)(128)(4,1)S(1)}, s32[]{:S(2)}) async-start(s8[9437184]{0:T(1024)(128)(4,1)} %bitcast.447), calls=%async_computation.2 | async-start | bytes 8388608
  346.8 29.2 %collective-permute-start.14 = (bf16[4,2,24,3072]{3,2,0,1:T(8,128)(2,1)}, bf16[4,2,24,3072]{3,2,0,1:T(8,128)(2,1)}, u32[]{:S(2)}, u32[]{:S(2)}) collective-permute-start(bf16[4,2,24,3072]{3,2,0,1:T(8,128)(2,1)} %dynamic-slice_bitcast_fusion.3), channel_id=1, source_target_pairs={{0,4},{1,5},{2,6},{3,7},{4,0},{5,1},{6,2},{7,3},{8,12},{9,13},{10,... | collective-permute-start | bytes 3538952 | tf_op jit(solution)/shard_map/ppermute | solution.py:43
  349.4 29.9 %collective-permute-start.16 = (bf16[4,2,24,3072]{3,2,0,1:T(8,128)(2,1)}, bf16[4,2,24,3072]{3,2,0,1:T(8,128)(2,1)}, u32[]{:S(2)}, u32[]{:S(2)}) collective-permute-start(bf16[4,2,24,3072]{3,2,0,1:T(8,128)(2,1)} %dynamic-slice_bitcast_fusion.2), channel_id=1, source_target_pairs={{0,2},{1,3},{2,0},{3,1},{4,6},{5,7},{6,4},{7,5},{8,10},{9,11},{10,... | collective-permute-start | bytes 3538952 | tf_op jit(solution)/shard_map/ppermute | solution.py:43
  354.8 46.4 %collective-permute-start.22 = (bf16[4,2,24,3072]{3,2,0,1:T(8,128)(2,1)S(1)}, bf16[4,2,24,3072]{3,2,0,1:T(8,128)(2,1)S(1)}, u32[]{:S(2)}, u32[]{:S(2)}) collective-permute-start(bf16[4,2,24,3072]{3,2,0,1:T(8,128)(2,1)S(1)} %bitcast.472), channel_id=1, source_target_pairs={{0,4},{1,5},{2,6},{3,7},{4,0},{5,1},{6,2},{7,3},{8,12},{9,13},{10,... | collective-permute-start | bytes 3538952 | tf_op jit(solution)/shard_map/ppermute | solution.py:43
  356.5 47.3 %collective-permute-start.24 = (bf16[4,2,24,3072]{3,2,1,0:T(8,128)(2,1)S(1)}, bf16[4,2,24,3072]{3,2,1,0:T(8,128)(2,1)S(1)}, u32[]{:S(2)}, u32[]{:S(2)}) collective-permute-start(bf16[4,2,24,3072]{3,2,1,0:T(8,128)(2,1)S(1)} %dynamic-slice_bitcast_fusion.1), channel_id=1, source_target_pairs={{0,2},{1,3},{2,0},{3,1},{4,6},{5,7},{6,4},{7,5},{8,10},{9,11},{10,... | collective-permute-start | bytes 3538952 | tf_op jit(solution)/shard_map/ppermute | solution.py:43
  377.8 51.8 %collective-permute-start.15 = (bf16[4,24,3072]{2,1,0:T(8,128)(2,1)S(1)}, bf16[4,24,3072]{2,1,0:T(8,128)(2,1)S(1)}, u32[]{:S(2)}, u32[]{:S(2)}) collective-permute-start(bf16[4,24,3072]{2,1,0:T(8,128)(2,1)S(1)} %dynamic-slice_bitcast_fusion.7), channel_id=1, source_target_pairs={{0,2},{1,3},{2,0},{3,1},{4,6},{5,7},{6,4},{7,5},{8,10},{9,11},{10,... | collective-permute-start | bytes 1769480 | tf_op jit(solution)/shard_map/ppermute | solution.py:43
  381.0 48.7 %collective-permute-start.17 = (bf16[4,24,3072]{2,1,0:T(8,128)(2,1)S(1)}, bf16[4,24,3072]{2,1,0:T(8,128)(2,1)S(1)}, u32[]{:S(2)}, u32[]{:S(2)}) collective-permute-start(bf16[4,24,3072]{2,1,0:T(8,128)(2,1)S(1)} %dynamic-slice_bitcast_fusion.6), channel_id=1, source_target_pairs={{0,4},{1,5},{2,6},{3,7},{4,0},{5,1},{6,2},{7,3},{8,12},{9,13},{10,... | collective-permute-start | bytes 1769480 | tf_op jit(solution)/shard_map/ppermute | solution.py:43
  401.7 23.0 %collective-permute-start.23 = (bf16[4,24,3072]{2,1,0:T(8,128)(2,1)S(1)}, bf16[4,24,3072]{2,1,0:T(8,128)(2,1)S(1)}, u32[]{:S(2)}, u32[]{:S(2)}) collective-permute-start(bf16[4,24,3072]{2,1,0:T(8,128)(2,1)S(1)} %dynamic-slice_bitcast_fusion.5), channel_id=1, source_target_pairs={{0,2},{1,3},{2,0},{3,1},{4,6},{5,7},{6,4},{7,5},{8,10},{9,11},{10,... | collective-permute-start | bytes 1769480 | tf_op jit(solution)/shard_map/ppermute | solution.py:43
  404.3 20.6 %collective-permute-start.25 = (bf16[4,24,3072]{2,1,0:T(8,128)(2,1)S(1)}, bf16[4,24,3072]{2,1,0:T(8,128)(2,1)S(1)}, u32[]{:S(2)}, u32[]{:S(2)}) collective-permute-start(bf16[4,24,3072]{2,1,0:T(8,128)(2,1)S(1)} %dynamic-slice_bitcast_fusion.4), channel_id=1, source_target_pairs={{0,4},{1,5},{2,6},{3,7},{4,0},{5,1},{6,2},{7,3},{8,12},{9,13},{10,... | collective-permute-start | bytes 1769480 | tf_op jit(solution)/shard_map/ppermute | solution.py:43
  425.1 11.8 %collective-permute-start.28 = (bf16[24,6144]{1,0:T(8,128)(2,1)S(1)}, bf16[24,6144]{1,0:T(8,128)(2,1)S(1)}, u32[]{:S(2)}, u32[]{:S(2)}) collective-permute-start(bf16[24,6144]{1,0:T(8,128)(2,1)S(1)} %get-tuple-element.159), channel_id=1, source_target_pairs={{0,24},{1,25},{2,26},{3,27},{4,28},{5,29},{6,30},{7,31},{8,16},{9,... | collective-permute-start | bytes 884744 | tf_op jit(solution)/shard_map/ppermute | solution.py:43
  427.5 36.0 %collective-permute-start.27 = (bf16[24,6144]{1,0:T(8,128)(2,1)S(1)}, bf16[24,6144]{1,0:T(8,128)(2,1)S(1)}, u32[]{:S(2)}, u32[]{:S(2)}) collective-permute-start(bf16[24,6144]{1,0:T(8,128)(2,1)S(1)} %get-tuple-element.158), channel_id=1, source_target_pairs={{0,16},{1,17},{2,18},{3,19},{4,20},{5,21},{6,22},{7,23},{8,24},{9,... | collective-permute-start | bytes 884744 | tf_op jit(solution)/shard_map/ppermute | solution.py:43
  428.3 35.2 %collective-permute-start.26 = (bf16[24,6144]{1,0:T(8,128)(2,1)S(1)}, bf16[24,6144]{1,0:T(8,128)(2,1)S(1)}, u32[]{:S(2)}, u32[]{:S(2)}) collective-permute-start(bf16[24,6144]{1,0:T(8,128)(2,1)S(1)} %get-tuple-element.157), channel_id=1, source_target_pairs={{0,8},{1,9},{2,10},{3,11},{4,12},{5,13},{6,14},{7,15},{8,0},{9,1},... | collective-permute-start | bytes 884744 | tf_op jit(solution)/shard_map/ppermute | solution.py:43
  430.0 34.5 %collective-permute-start.20 = (bf16[24,6144]{1,0:T(8,128)(2,1)S(1)}, bf16[24,6144]{1,0:T(8,128)(2,1)S(1)}, u32[]{:S(2)}, u32[]{:S(2)}) collective-permute-start(bf16[24,6144]{1,0:T(8,128)(2,1)S(1)} %get-tuple-element.162), channel_id=1, source_target_pairs={{0,24},{1,25},{2,26},{3,27},{4,28},{5,29},{6,30},{7,31},{8,16},{9,... | collective-permute-start | bytes 884744 | tf_op jit(solution)/shard_map/ppermute | solution.py:43
  432.3 42.6 %collective-permute-start.19 = (bf16[24,6144]{1,0:T(8,128)(2,1)S(1)}, bf16[24,6144]{1,0:T(8,128)(2,1)S(1)}, u32[]{:S(2)}, u32[]{:S(2)}) collective-permute-start(bf16[24,6144]{1,0:T(8,128)(2,1)S(1)} %get-tuple-element.161), channel_id=1, source_target_pairs={{0,16},{1,17},{2,18},{3,19},{4,20},{5,21},{6,22},{7,23},{8,24},{9,... | collective-permute-start | bytes 884744 | tf_op jit(solution)/shard_map/ppermute | solution.py:43
  436.9 38.0 %collective-permute-start.18 = (bf16[24,6144]{1,0:T(8,128)(2,1)S(1)}, bf16[24,6144]{1,0:T(8,128)(2,1)S(1)}, u32[]{:S(2)}, u32[]{:S(2)}) collective-permute-start(bf16[24,6144]{1,0:T(8,128)(2,1)S(1)} %get-tuple-element.160), channel_id=1, source_target_pairs={{0,8},{1,9},{2,10},{3,11},{4,12},{5,13},{6,14},{7,15},{8,0},{9,1},... | collective-permute-start | bytes 884744 | tf_op jit(solution)/shard_map/ppermute | solution.py:43
  (27 other events, 87.1 us)
Sparse Core Ops, SparseCore 0:
  22.9 129.0 all-gather.1
